TPU v7x, 32 devices: a whole 2x2x4 slice. The times are simulated.
32 devices in a mesh: row: 8 (over z, x), col: 4 (over y, core).
Axes of the slice: x: 2, y: 2, z: 4, core: 2. Of those that a mesh axis runs over, the one named last changes fastest.
Arguments:
- level_cot: float32 [128, 256, 128], P('col', 'row'), may hold values from -6 to 6
- level_state: float32 [128, 256, 128], P('col', 'row'), may hold values from -6 to 6
- momentum_cot: float32 [3, 128, 256, 128], P(None, 'col', 'row'), may hold values from -6 to 6
- courant: float32 [128, 256, 128], P('col', 'row'), may hold values from 0.05 to 0.3
- stencil: int32 [128, 256, 128], P('col', 'row'), may hold values from 0 to 2
- upwind: int32 [128, 256, 128], P('col', 'row'), may hold values from 0 to 1
- viscosity: float32 [128, 256, 128], P('col', 'row'), may hold values from 0.3 to 3
- band_cells: int32 [4, 8, 4096], P('col', 'row'), may hold values from 1 to 131070, as said below
- band_count: int32 [4, 8], P('col', 'row'), may hold values from 1024 to 4096, as said below
- band_force: float32 [3, 4, 8, 4096], P(None, 'col', 'row'), may hold values from -6 to 6
- design_basis: float32 [16, 128, 256], P(None, 'col', 'row')
Outputs:
- level_adjoint: float32 [128, 256, 128], P('col', 'row')
- momentum_adjoint: float32 [3, 128, 256, 128], P(None, 'col', 'row')
- design_grad: float32 [8, 16], P('row')
Inputs may be any that keep to these rules, and one draw needn't show every extreme that they name: `band_count`: every nozzle's live band entries are at least 1024, and some nozzle has exactly 4096. `band_cells`: each entry is (x 32 + y) * 128 + z for a cell (x, y, z) of the nozzle's block with z from 1 to 126; cells may repeat.
All inputs are finite; a program needn't handle non-finite values.
Results may differ from a plain program's by a relative error of at most 0.00002.
Values sent between devices are 32-bit elements; how exact they have to be, the bound alone decides.
A program may use at most 192 MiB of HBM per device.

v0:
```python
import math

import jax
import jax.numpy as jnp
from jax import lax
from jax.sharding import PartitionSpec as P

SUBSTEPS = 6


candidate_weights = (
    (1.0 / 3.0, -7.0 / 6.0, 11.0 / 6.0, 0.0, 0.0, 0.0),
    (0.0, -1.0 / 6.0, 5.0 / 6.0, 1.0 / 3.0, 0.0, 0.0),
    (0.0, 0.0, 1.0 / 3.0, 5.0 / 6.0, -1.0 / 6.0, 0.0),
    (0.0, 0.0, 0.0, 11.0 / 6.0, -7.0 / 6.0, 1.0 / 3.0),
    (0.0, 0.0, 1.0 / 3.0, 5.0 / 6.0, -1.0 / 6.0, 0.0),
    (0.0, -1.0 / 6.0, 5.0 / 6.0, 1.0 / 3.0, 0.0, 0.0),
)
rate_value = 0.05


def extended(x, sides, width):
    for axis, dim in sides:
        count, length = (lax.axis_size(axis), x.shape[dim])
        up = [(i, (i + 1) % count) for i in range(count - 1)]
        down = [(j, i) for i, j in up]
        last = lax.slice_in_dim(x, length - width, length, axis=dim)
        initial = lax.slice_in_dim(x, 0, width, axis=dim)
        before = lax.ppermute(last, axis, up)
        after = lax.ppermute(initial, axis, down)
        x = jnp.concatenate([before, x, after], axis=dim)
    return x


def passed_along(x, axis, by):
    count = lax.axis_size(axis)
    pairs = [(i, i + by) for i in range(count) if 0 <= i + by < count]
    return lax.ppermute(x, axis, pairs)


def offset_weights(face_code):
    result = []
    for offset in range(6):
        accum = jnp.zeros(face_code.shape, jnp.float32)
        for candidate in range(6):
            value = candidate_weights[candidate][offset]
            if value != 0.0:
                accum = accum + jnp.where(face_code == candidate, value, 0.0).astype(jnp.float32)
        result.append(accum)
    return result


def diffuse(padded_field, padded_mu):
    centre = padded_field[:, 1:-1, 1:-1]
    mu_centre = padded_mu[1:-1, 1:-1]
    accum = jnp.zeros_like(centre)
    pairs = (
        (padded_field[:, 2:, 1:-1], padded_mu[2:, 1:-1]),
        (padded_field[:, :-2, 1:-1], padded_mu[:-2, 1:-1]),
        (padded_field[:, 1:-1, 2:], padded_mu[1:-1, 2:]),
        (padded_field[:, 1:-1, :-2], padded_mu[1:-1, :-2]),
    )
    for near_field, near_mu in pairs:
        accum = accum + 0.5 * (mu_centre + near_mu) * (near_field - centre)
    upper = jnp.pad(centre[..., 1:], ((0, 0), (0, 0), (0, 0), (0, 1)))
    lower = jnp.pad(centre[..., :-1], ((0, 0), (0, 0), (0, 0), (1, 0)))
    mu_upper = jnp.pad(mu_centre[..., 1:], ((0, 0), (0, 0), (0, 1)))
    mu_lower = jnp.pad(mu_centre[..., :-1], ((0, 0), (0, 0), (1, 0)))
    accum = accum + 0.5 * (mu_centre + mu_upper) * (upper - centre)
    accum = accum + 0.5 * (mu_centre + mu_lower) * (lower - centre)
    return accum


def local(
    level_cot,
    level_state,
    momentum_cot,
    courant,
    stencil,
    upwind,
    viscosity,
    band_cells,
    band_count,
    band_force,
    design_basis,
):
    width_x, width_y, depth_z = level_cot.shape
    total_x = width_x * lax.axis_size("col")
    start_x = lax.axis_index("col") * width_x
    state_ext, cot_ext = (
        extended(level_state, (("col", 0),), 3),
        extended(level_cot, (("col", 0),), 3),
    )
    face_code = stencil + 3 * upwind
    weights = offset_weights(face_code)
    inside = (start_x + jnp.arange(width_x) < total_x - 1)[:, None, None]
    face_speed = jnp.where(inside, courant * (1 - 2 * upwind).astype(jnp.float32), 0.0)
    cot_jump = cot_ext[4 : 4 + width_x] - level_cot
    weighted = cot_jump * face_speed
    spread = jnp.zeros((width_x + 5, width_y, depth_z), jnp.float32)
    for offset in range(6):
        spread = spread + jnp.pad(
            weighted * weights[offset], ((offset, 5 - offset), (0, 0), (0, 0))
        )
    from_right = passed_along(spread[:2], "col", -1)
    from_left = passed_along(spread[width_x + 2 :], "col", 1)
    returned = spread[2 : 2 + width_x].at[:3].add(from_left).at[width_x - 2 :].add(from_right)
    face_value = jnp.zeros_like(level_state)
    for offset in range(6):
        face_value = face_value + weights[offset] * state_ext[offset + 1 : offset + 1 + width_x]
    level_base = level_cot + returned
    band_index = band_cells[0, 0]
    is_live = jnp.arange(band_index.shape[0]) < band_count[0, 0]
    picked = jnp.take(momentum_cot.reshape(3, -1), band_index, axis=1)
    strength = jnp.where(is_live, jnp.sum(band_force[:, 0, 0, :] * picked, axis=0), 0.0)
    level_flat = level_base.reshape(-1)
    level_flat = level_flat.at[band_index].add(-2.0 * strength)
    level_flat = level_flat.at[band_index + 1].add(strength)
    level_flat = level_flat.at[band_index - 1].add(strength)
    level_adjoint = level_flat.reshape(width_x, width_y, depth_z)
    momentum = momentum_cot
    padded_mu = extended(viscosity, (("row", 1), ("col", 0)), 1)
    for substep in range(SUBSTEPS):
        padded_field = extended(momentum, (("row", 2), ("col", 1)), 1)
        momentum = momentum + rate_value * diffuse(padded_field, padded_mu)
    sensitivity = jnp.sum(cot_jump * face_value * face_speed, axis=2)
    partial_value = jnp.sum(design_basis * sensitivity[None], axis=(1, 2))
    summed = lax.psum(partial_value, "col")
    design_grad = (summed / math.sqrt(total_x * width_y * depth_z)).reshape(1, -1)
    return (level_adjoint, momentum, design_grad)


def solution(mesh):
    placed = (
        P("col", "row", None),
        P("col", "row", None),
        P(None, "col", "row", None),
        P("col", "row", None),
        P("col", "row", None),
        P("col", "row", None),
        P("col", "row", None),
        P("col", "row", None),
        P("col", "row"),
        P(None, "col", "row", None),
        P(None, "col", "row"),
    )
    return jax.shard_map(
        local,
        mesh=mesh,
        in_specs=placed,
        out_specs=(P("col", "row", None), P(None, "col", "row", None), P("row", None)),
        check_vma=False,
    )
```

profile of v0, /device:TPU:9, one launch (start us, length us, event | category | flops | bytes accessed | tf_op | source)
XLA Modules:
  0.0 321.2 jit_solution(544238155759930395)
XLA Ops:
  2.4 3.1 collective-permute-start.3
  5.5 3.1 collective-permute-start.4
  10.4 2.2 collective-permute-start.6
  12.6 4.0 %collective-permute-start.7 = (f32[3,32,1,128]{3,2,1,0:T(1,128)S(1)}, f32[3,32,1,128]{3,2,1,0:T(1,128)S(1)}, u32[]{:S(2)}, u32[]{:S(2)}) collective-permute-start(f32[3,32,1,128]{3,2,1,0:T(1,128)S(1)} %get-tuple-element.72), channel_id=1, source_target_pairs={{4,0},{8,4},{12,8},{16,12},{20,16},{24,20},{28,24},{5,1},{9,5},{13... | collective-permute-start | bytes 147464 | tf_op jit(solution)/shard_map/ppermute | solution.py:30
  17.4 4.8 %collective-permute-start.31 = (f32[3,32,128]{2,1,0:T(8,128)S(1)}, f32[3,32,128]{2,1,0:T(8,128)S(1)}, u32[]{:S(2)}, u32[]{:S(2)}) collective-permute-start(f32[3,32,128]{2,1,0:T(8,128)S(1)} %get-tuple-element.93), channel_id=1, source_target_pairs={{0,1},{1,2},{2,3},{4,5},{5,6},{6,7},{8,9},{9,10},{10,11},{12,13},{... | collective-permute-start | bytes 147464 | tf_op jit(solution)/shard_map/ppermute | solution.py:29
  22.2 2.2 fusion.131
  24.4 2.2 fusion.128
  26.6 31.9 %copy.17 = f32[3,32,32,128]{0,3,2,1:T(8,128)} copy(f32[3,32,32,128]{3,2,1,0:T(8,128)S(1)} %copy-done.1) | data formatting | bytes 3145728 | tf_op args[2]
  58.6 2.0 copy.16
  61.8 59.8 %gather_fusion = f32[4096,3]{1,0:T(8,128)} fusion(f32[3,131072]{0,1:T(8,128)} %bitcast.6, s32[4096]{0:T(1024)S(1)} %broadcast_clamp_fusion), kind=kCustom, calls=%fused_computation | custom fusion | bytes 114688 | tf_op jit(solution)/shard_map/jit(_take)/gather | solution.py:114
  121.6 2.9 fusion
  124.6 1.9 collective-permute-start.5
  126.5 3.6 %collective-permute-start.9 = (f32[1,34,128]{2,1,0:T(8,128)S(1)}, f32[1,34,128]{2,1,0:T(8,128)S(1)}, u32[]{:S(2)}, u32[]{:S(2)}) collective-permute-start(f32[1,34,128]{2,1,0:T(8,128)S(1)} %get-tuple-element.82), channel_id=1, source_target_pairs={{0,1},{1,2},{2,3},{4,5},{5,6},{6,7},{8,9},{9,10},{10,11},{12,13},{... | collective-permute-start | bytes 52232 | tf_op jit(solution)/shard_map/ppermute | solution.py:29
  130.2 1.9 collective-permute-start.32
  132.1 1.9 collective-permute-start
  135.8 3.9 %collective-permute-start.10 = (f32[3,1,34,128]{3,2,1,0:T(8,128)S(1)}, f32[3,1,34,128]{3,2,1,0:T(8,128)S(1)}, u32[]{:S(2)}, u32[]{:S(2)}) collective-permute-start(f32[3,1,34,128]{3,2,1,0:T(8,128)S(1)} %get-tuple-element.49), channel_id=1, source_target_pairs={{0,1},{1,2},{2,3},{4,5},{5,6},{6,7},{8,9},{9,10},{10,11},{12,13},{... | collective-permute-start | bytes 156680 | tf_op jit(solution)/shard_map/ppermute | solution.py:29
  139.7 1.9 collective-permute-start.8
  145.8 2.2 collective-permute-start.2
  148.0 3.6 %collective-permute-start.1 = (f32[3,32,128]{2,1,0:T(8,128)S(1)}, f32[3,32,128]{2,1,0:T(8,128)S(1)}, u32[]{:S(2)}, u32[]{:S(2)}) collective-permute-start(f32[3,32,128]{2,1,0:T(8,128)S(1)} %pad_add_fusion.1), channel_id=1, source_target_pairs={{0,1},{1,2},{2,3},{4,5},{5,6},{6,7},{8,9},{9,10},{10,11},{12,13},{... | collective-permute-start | bytes 147464 | tf_op jit(solution)/shard_map/ppermute | solution.py:38
  151.7 2.6 fusion.82
  154.4 1.9 collective-permute-start.11
  156.3 4.3 %collective-permute-start.12 = (f32[3,32,1,128]{3,2,1,0:T(1,128)S(1)}, f32[3,32,1,128]{3,2,1,0:T(1,128)S(1)}, u32[]{:S(2)}, u32[]{:S(2)}) collective-permute-start(f32[3,32,1,128]{3,2,1,0:T(1,128)S(1)} %get-tuple-element.68), channel_id=1, source_target_pairs={{4,0},{8,4},{12,8},{16,12},{20,16},{24,20},{28,24},{5,1},{9,5},{13... | collective-permute-start | bytes 147464 | tf_op jit(solution)/shard_map/ppermute | solution.py:30
  160.8 5.1 %psum.7 = f32[16]{0:T(128)S(1)} all-reduce(f32[16]{0:T(128)S(1)} %multiply_reduce_fusion), channel_id=1, replica_groups=mesh['row'=8,'col'=4] {'col'}, use_global_device_ids=true, to_apply=%region_6.7 | all-reduce | flops 16 | bytes 128 | tf_op jit(solution)/shard_map/psum | solution.py:128
  165.9 3.0 collective-permute-start.13
  169.0 3.4 %collective-permute-start.14 = (f32[3,1,34,128]{3,2,1,0:T(8,128)S(1)}, f32[3,1,34,128]{3,2,1,0:T(8,128)S(1)}, u32[]{:S(2)}, u32[]{:S(2)}) collective-permute-start(f32[3,1,34,128]{3,2,1,0:T(8,128)S(1)} %get-tuple-element.47), channel_id=1, source_target_pairs={{0,1},{1,2},{2,3},{4,5},{5,6},{6,7},{8,9},{9,10},{10,11},{12,13},{... | collective-permute-start | bytes 156680 | tf_op jit(solution)/shard_map/ppermute | solution.py:29
  173.7 2.6 fusion.67
  176.3 2.1 collective-permute-start.15
  178.4 4.1 %collective-permute-start.16 = (f32[3,32,1,128]{3,2,1,0:T(1,128)S(1)}, f32[3,32,1,128]{3,2,1,0:T(1,128)S(1)}, u32[]{:S(2)}, u32[]{:S(2)}) collective-permute-start(f32[3,32,1,128]{3,2,1,0:T(1,128)S(1)} %get-tuple-element.64), channel_id=1, source_target_pairs={{4,0},{8,4},{12,8},{16,12},{20,16},{24,20},{28,24},{5,1},{9,5},{13... | collective-permute-start | bytes 147464 | tf_op jit(solution)/shard_map/ppermute | solution.py:30
  184.2 1.9 collective-permute-start.17
  186.1 5.6 %collective-permute-start.18 = (f32[3,1,34,128]{3,2,1,0:T(8,128)S(1)}, f32[3,1,34,128]{3,2,1,0:T(8,128)S(1)}, u32[]{:S(2)}, u32[]{:S(2)}) collective-permute-start(f32[3,1,34,128]{3,2,1,0:T(8,128)S(1)} %get-tuple-element.45), channel_id=1, source_target_pairs={{0,1},{1,2},{2,3},{4,5},{5,6},{6,7},{8,9},{9,10},{10,11},{12,13},{... | collective-permute-start | bytes 156680 | tf_op jit(solution)/shard_map/ppermute | solution.py:29
  192.8 2.5 fusion.52
  195.5 4.5 %collective-permute-start.19 = (f32[3,32,1,128]{3,2,1,0:T(1,128)S(1)}, f32[3,32,1,128]{3,2,1,0:T(1,128)S(1)}, u32[]{:S(2)}, u32[]{:S(2)}) collective-permute-start(f32[3,32,1,128]{3,2,1,0:T(1,128)S(1)} %get-tuple-element.61), channel_id=1, source_target_pairs={{0,4},{4,8},{8,12},{12,16},{16,20},{20,24},{24,28},{1,5},{5,9},{9,... | collective-permute-start | bytes 147464 | tf_op jit(solution)/shard_map/ppermute | solution.py:29
  200.0 1.9 collective-permute-start.20
  202.4 2.5 collective-permute-done.20
  204.9 1.9 collective-permute-start.21
  206.8 5.7 %collective-permute-start.22 = (f32[3,1,34,128]{3,2,1,0:T(8,128)S(1)}, f32[3,1,34,128]{3,2,1,0:T(8,128)S(1)}, u32[]{:S(2)}, u32[]{:S(2)}) collective-permute-start(f32[3,1,34,128]{3,2,1,0:T(8,128)S(1)} %get-tuple-element.43), channel_id=1, source_target_pairs={{0,1},{1,2},{2,3},{4,5},{5,6},{6,7},{8,9},{9,10},{10,11},{12,13},{... | collective-permute-start | bytes 156680 | tf_op jit(solution)/shard_map/ppermute | solution.py:29
  213.8 2.5 fusion.37
  216.4 2.6 collective-permute-start.23
  218.9 3.6 %collective-permute-start.24 = (f32[3,32,1,128]{3,2,1,0:T(1,128)S(1)}, f32[3,32,1,128]{3,2,1,0:T(1,128)S(1)}, u32[]{:S(2)}, u32[]{:S(2)}) collective-permute-start(f32[3,32,1,128]{3,2,1,0:T(1,128)S(1)} %get-tuple-element.56), channel_id=1, source_target_pairs={{4,0},{8,4},{12,8},{16,12},{20,16},{24,20},{28,24},{5,1},{9,5},{13... | collective-permute-start | bytes 147464 | tf_op jit(solution)/shard_map/ppermute | solution.py:30
  224.1 1.9 collective-permute-start.25
  226.0 5.4 %collective-permute-start.26 = (f32[3,1,34,128]{3,2,1,0:T(8,128)S(1)}, f32[3,1,34,128]{3,2,1,0:T(8,128)S(1)}, u32[]{:S(2)}, u32[]{:S(2)}) collective-permute-start(f32[3,1,34,128]{3,2,1,0:T(8,128)S(1)} %get-tuple-element.41), channel_id=1, source_target_pairs={{0,1},{1,2},{2,3},{4,5},{5,6},{6,7},{8,9},{9,10},{10,11},{12,13},{... | collective-permute-start | bytes 156680 | tf_op jit(solution)/shard_map/ppermute | solution.py:29
  232.7 2.5 fusion.22
  235.3 4.5 %collective-permute-start.27 = (f32[3,32,1,128]{3,2,1,0:T(1,128)S(1)}, f32[3,32,1,128]{3,2,1,0:T(1,128)S(1)}, u32[]{:S(2)}, u32[]{:S(2)}) collective-permute-start(f32[3,32,1,128]{3,2,1,0:T(1,128)S(1)} %get-tuple-element.53), channel_id=1, source_target_pairs={{0,4},{4,8},{8,12},{12,16},{16,20},{20,24},{24,28},{1,5},{5,9},{9,... | collective-permute-start | bytes 147464 | tf_op jit(solution)/shard_map/ppermute | solution.py:29
  241.9 22.6 %scatter_fusion = f32[131072]{0:T(1024)S(1)} fusion(f32[131072]{0:T(1024)S(1)} %bitcast.31, s32[4096]{0:T(1024)S(1)} %bitcast.34, f32[4096]{0:T(1024)S(1)} %get-tuple-element.34), kind=kCustom, calls=%fused_computation.1 | custom fusion | flops 4096 | bytes 65536 | tf_op jit(solution)/shard_map/scatter-add | solution.py:117
  264.5 22.6 %scatter_fusion.1 = f32[131072]{0:T(1024)S(1)} fusion(f32[131072]{0:T(1024)S(1)} %scatter_fusion, s32[4096]{0:T(1024)S(1)} %bitcast.36, f32[4096]{0:T(1024)S(1)} %get-tuple-element.35), kind=kCustom, calls=%fused_computation.2 | custom fusion | flops 4096 | bytes 65536 | tf_op jit(solution)/shard_map/scatter-add | solution.py:118
  287.2 22.6 %scatter_fusion.2 = f32[131072]{0:T(1024)S(1)} fusion(f32[131072]{0:T(1024)S(1)} %scatter_fusion.1, s32[4096]{0:T(1024)S(1)} %bitcast.35, f32[4096]{0:T(1024)S(1)} %get-tuple-element.35), kind=kCustom, calls=%fused_computation.3 | custom fusion | flops 4096 | bytes 65536 | tf_op jit(solution)/shard_map/scatter-add | solution.py:119
  311.8 4.7 %collective-permute-start.30 = (f32[3,1,34,128]{3,2,1,0:T(8,128)S(1)}, f32[3,1,34,128]{3,2,1,0:T(8,128)S(1)}, u32[]{:S(2)}, u32[]{:S(2)}) collective-permute-start(f32[3,1,34,128]{3,2,1,0:T(8,128)S(1)} %get-tuple-element.39), channel_id=1, source_target_pairs={{0,1},{1,2},{2,3},{4,5},{5,6},{6,7},{8,9},{9,10},{10,11},{12,13},{... | collective-permute-start | bytes 156680 | tf_op jit(solution)/shard_map/ppermute | solution.py:29
  317.8 3.4 %fusion.7 = f32[3,32,32,128]{3,2,1,0:T(8,128)} fusion(f32[3,32,32,128]{3,2,1,0:T(8,128)S(1)} %fusion.22, f32[3,32,1,128]{3,2,1,0:T(1,128)S(1)} %collective-permute-done.27, f32[3,32,1,128]{3,2,1,0:T(1,128)S(1)} %collective-permute-done.28, f32[3,1,34,128]{3,2,1,0:T(8,128)S(1)} %collective-permute-done.30, f32[3,1,34,128]{3,2,1,0:T(8,128)S(1)} %collective-permute-done.29, ...), kind=kLoop, calls=%fused_computation.13 | loop fusion | flops 10616832 | bytes 9615360 | tf_op jit(solution)/shard_map/add | solution.py:125
  (163 shorter events, 24.9 us)
Async XLA Ops:
  0.6 23.7 %copy-start.1 = (f32[3,32,32,128]{3,2,1,0:T(8,128)S(1)}, f32[3,32,32,128]{3,2,1,0:T(8,128)}, u32[]{:S(2)}) copy-start(f32[3,32,32,128]{3,2,1,0:T(8,128)} %param.17) | copy-start | bytes 4718596
  2.4 122.2 %collective-permute-start.3 = (f32[32,1,128]{2,1,0:T(1,128)}, f32[32,1,128]{2,1,0:T(1,128)S(1)}, u32[]{:S(2)}, u32[]{:S(2)}) collective-permute-start(f32[32,1,128]{2,1,0:T(1,128)} %get-tuple-element.88), channel_id=1, source_target_pairs={{0,4},{4,8},{8,12},{12,16},{16,20},{20,24},{24,28},{1,5},{5,9},{9,... | collective-permute-start | bytes 49160 | tf_op jit(solution)/shard_map/ppermute | solution.py:29
  5.5 119.0 %collective-permute-start.4 = (f32[32,1,128]{2,1,0:T(1,128)}, f32[32,1,128]{2,1,0:T(1,128)S(1)}, u32[]{:S(2)}, u32[]{:S(2)}) collective-permute-start(f32[32,1,128]{2,1,0:T(1,128)} %get-tuple-element.87), channel_id=1, source_target_pairs={{4,0},{8,4},{12,8},{16,12},{20,16},{24,20},{28,24},{5,1},{9,5},{13... | collective-permute-start | bytes 49160 | tf_op jit(solution)/shard_map/ppermute | solution.py:30
  10.4 125.4 %collective-permute-start.6 = (f32[3,32,1,128]{3,2,1,0:T(1,128)}, f32[3,32,1,128]{3,2,1,0:T(1,128)S(1)}, u32[]{:S(2)}, u32[]{:S(2)}) collective-permute-start(f32[3,32,1,128]{3,2,1,0:T(1,128)} %get-tuple-element.73), channel_id=1, source_target_pairs={{0,4},{4,8},{8,12},{12,16},{16,20},{20,24},{24,28},{1,5},{5,9},{9,... | collective-permute-start | bytes 147464 | tf_op jit(solution)/shard_map/ppermute | solution.py:29
  12.6 123.2 %collective-permute-start.7 = (f32[3,32,1,128]{3,2,1,0:T(1,128)S(1)}, f32[3,32,1,128]{3,2,1,0:T(1,128)S(1)}, u32[]{:S(2)}, u32[]{:S(2)}) collective-permute-start(f32[3,32,1,128]{3,2,1,0:T(1,128)S(1)} %get-tuple-element.72), channel_id=1, source_target_pairs={{4,0},{8,4},{12,8},{16,12},{20,16},{24,20},{28,24},{5,1},{9,5},{13... | collective-permute-start | bytes 147464 | tf_op jit(solution)/shard_map/ppermute | solution.py:30
  17.4 124.2 %collective-permute-start.31 = (f32[3,32,128]{2,1,0:T(8,128)S(1)}, f32[3,32,128]{2,1,0:T(8,128)S(1)}, u32[]{:S(2)}, u32[]{:S(2)}) collective-permute-start(f32[3,32,128]{2,1,0:T(8,128)S(1)} %get-tuple-element.93), channel_id=1, source_target_pairs={{0,1},{1,2},{2,3},{4,5},{5,6},{6,7},{8,9},{9,10},{10,11},{12,13},{... | collective-permute-start | bytes 147464 | tf_op jit(solution)/shard_map/ppermute | solution.py:29
  26.6 31.9 %copy-start.41 = (s32[1,1,4096]{2,1,0:T(1,128)S(1)}, s32[1,1,4096]{2,1,0:T(1,128)}, u32[]{:S(2)}) copy-start(s32[1,1,4096]{2,1,0:T(1,128)} %param.22) | copy-start | bytes 49156
  26.6 31.9 %copy-start.42 = (f32[3,1,1,4096]{3,2,1,0:T(1,128)S(1)}, f32[3,1,1,4096]{3,2,1,0:T(1,128)}, u32[]{:S(2)}) copy-start(f32[3,1,1,4096]{3,2,1,0:T(1,128)} %param.24) | copy-start | bytes 147460
  124.6 5.6 %collective-permute-start.5 = (f32[1,34,128]{2,1,0:T(8,128)S(1)}, f32[1,34,128]{2,1,0:T(8,128)S(1)}, u32[]{:S(2)}, u32[]{:S(2)}) collective-permute-start(f32[1,34,128]{2,1,0:T(8,128)S(1)} %get-tuple-element.81), channel_id=1, source_target_pairs={{1,0},{2,1},{3,2},{5,4},{6,5},{7,6},{9,8},{10,9},{11,10},{13,12},{... | collective-permute-start | bytes 52232 | tf_op jit(solution)/shard_map/ppermute | solution.py:30
  126.5 5.6 %collective-permute-start.9 = (f32[1,34,128]{2,1,0:T(8,128)S(1)}, f32[1,34,128]{2,1,0:T(8,128)S(1)}, u32[]{:S(2)}, u32[]{:S(2)}) collective-permute-start(f32[1,34,128]{2,1,0:T(8,128)S(1)} %get-tuple-element.82), channel_id=1, source_target_pairs={{0,1},{1,2},{2,3},{4,5},{5,6},{6,7},{8,9},{9,10},{10,11},{12,13},{... | collective-permute-start | bytes 52232 | tf_op jit(solution)/shard_map/ppermute | solution.py:29
  130.2 11.6 %collective-permute-start.32 = (f32[3,32,128]{2,1,0:T(8,128)S(1)}, f32[3,32,128]{2,1,0:T(8,128)S(1)}, u32[]{:S(2)}, u32[]{:S(2)}) collective-permute-start(f32[3,32,128]{2,1,0:T(8,128)S(1)} %get-tuple-element.94), channel_id=1, source_target_pairs={{1,0},{2,1},{3,2},{5,4},{6,5},{7,6},{9,8},{10,9},{11,10},{13,12},{... | collective-permute-start | bytes 147464 | tf_op jit(solution)/shard_map/ppermute | solution.py:30
  132.1 9.7 %collective-permute-start = (f32[3,32,128]{2,1,0:T(8,128)S(1)}, f32[3,32,128]{2,1,0:T(8,128)S(1)}, u32[]{:S(2)}, u32[]{:S(2)}) collective-permute-start(f32[3,32,128]{2,1,0:T(8,128)S(1)} %slice.359), channel_id=1, source_target_pairs={{1,0},{2,1},{3,2},{5,4},{6,5},{7,6},{9,8},{10,9},{11,10},{13,12},{... | collective-permute-start | bytes 147464 | tf_op jit(solution)/shard_map/ppermute | solution.py:30
  135.6 16.0 %copy-start.2 = (f32[32,32,128]{2,1,0:T(8,128)}, f32[32,32,128]{2,1,0:T(8,128)S(1)}, u32[]{:S(2)}) copy-start(f32[32,32,128]{2,1,0:T(8,128)S(1)} %get-tuple-element.79) | copy-start | bytes 1572868
  135.6 16.0 %copy-start.4 = (f32[32,32,128]{2,1,0:T(8,128)}, f32[32,32,128]{2,1,0:T(8,128)S(1)}, u32[]{:S(2)}) copy-start(f32[32,32,128]{2,1,0:T(8,128)S(1)} %get-tuple-element.80) | copy-start | bytes 1572868
  135.6 16.0 %copy-start.6 = (f32[32,32,128]{2,1,0:T(8,128)}, f32[32,32,128]{2,1,0:T(8,128)S(1)}, u32[]{:S(2)}) copy-start(f32[32,32,128]{2,1,0:T(8,128)S(1)} %get-tuple-element.83) | copy-start | bytes 1572868
  135.7 16.0 %copy-start.9 = (f32[32,32,128]{2,1,0:T(8,128)}, f32[32,32,128]{2,1,0:T(8,128)S(1)}, u32[]{:S(2)}) copy-start(f32[32,32,128]{2,1,0:T(8,128)S(1)} %get-tuple-element.84) | copy-start | bytes 1572868
  135.7 16.0 %copy-start.12 = (f32[32,32,128]{2,1,0:T(8,128)}, f32[32,32,128]{2,1,0:T(8,128)S(1)}, u32[]{:S(2)}) copy-start(f32[32,32,128]{2,1,0:T(8,128)S(1)} %get-tuple-element.85) | copy-start | bytes 1572868
  135.7 16.0 %copy-start.15 = (f32[32,32,128]{2,1,0:T(8,128)}, f32[32,32,128]{2,1,0:T(8,128)S(1)}, u32[]{:S(2)}) copy-start(f32[32,32,128]{2,1,0:T(8,128)S(1)} %get-tuple-element.86) | copy-start | bytes 1572868
  135.8 15.9 %collective-permute-start.10 = (f32[3,1,34,128]{3,2,1,0:T(8,128)S(1)}, f32[3,1,34,128]{3,2,1,0:T(8,128)S(1)}, u32[]{:S(2)}, u32[]{:S(2)}) collective-permute-start(f32[3,1,34,128]{3,2,1,0:T(8,128)S(1)} %get-tuple-element.49), channel_id=1, source_target_pairs={{0,1},{1,2},{2,3},{4,5},{5,6},{6,7},{8,9},{9,10},{10,11},{12,13},{... | collective-permute-start | bytes 156680 | tf_op jit(solution)/shard_map/ppermute | solution.py:29
  139.7 11.9 %collective-permute-start.8 = (f32[3,1,34,128]{3,2,1,0:T(8,128)S(1)}, f32[3,1,34,128]{3,2,1,0:T(8,128)S(1)}, u32[]{:S(2)}, u32[]{:S(2)}) collective-permute-start(f32[3,1,34,128]{3,2,1,0:T(8,128)S(1)} %get-tuple-element.48), channel_id=1, source_target_pairs={{1,0},{2,1},{3,2},{5,4},{6,5},{7,6},{9,8},{10,9},{11,10},{13,12},{... | collective-permute-start | bytes 156680 | tf_op jit(solution)/shard_map/ppermute | solution.py:30
  145.8 96.0 %collective-permute-start.2 = (f32[2,32,128]{2,1,0:T(8,128)S(1)}, f32[2,32,128]{2,1,0:T(8,128)S(1)}, u32[]{:S(2)}, u32[]{:S(2)}) collective-permute-start(f32[2,32,128]{2,1,0:T(8,128)S(1)} %pad_add_fusion.2), channel_id=1, source_target_pairs={{1,0},{2,1},{3,2},{5,4},{6,5},{7,6},{9,8},{10,9},{11,10},{13,12},{... | collective-permute-start | bytes 98312 | tf_op jit(solution)/shard_map/ppermute | solution.py:38
  148.0 74.6 %collective-permute-start.1 = (f32[3,32,128]{2,1,0:T(8,128)S(1)}, f32[3,32,128]{2,1,0:T(8,128)S(1)}, u32[]{:S(2)}, u32[]{:S(2)}) collective-permute-start(f32[3,32,128]{2,1,0:T(8,128)S(1)} %pad_add_fusion.1), channel_id=1, source_target_pairs={{0,1},{1,2},{2,3},{4,5},{5,6},{6,7},{8,9},{9,10},{10,11},{12,13},{... | collective-permute-start | bytes 147464 | tf_op jit(solution)/shard_map/ppermute | solution.py:38
  154.4 11.5 %collective-permute-start.11 = (f32[3,32,1,128]{3,2,1,0:T(1,128)S(1)}, f32[3,32,1,128]{3,2,1,0:T(1,128)S(1)}, u32[]{:S(2)}, u32[]{:S(2)}) collective-permute-start(f32[3,32,1,128]{3,2,1,0:T(1,128)S(1)} %get-tuple-element.69), channel_id=1, source_target_pairs={{0,4},{4,8},{8,12},{12,16},{16,20},{20,24},{24,28},{1,5},{5,9},{9,... | collective-permute-start | bytes 147464 | tf_op jit(solution)/shard_map/ppermute | solution.py:29
  156.3 9.6 %collective-permute-start.12 = (f32[3,32,1,128]{3,2,1,0:T(1,128)S(1)}, f32[3,32,1,128]{3,2,1,0:T(1,128)S(1)}, u32[]{:S(2)}, u32[]{:S(2)}) collective-permute-start(f32[3,32,1,128]{3,2,1,0:T(1,128)S(1)} %get-tuple-element.68), channel_id=1, source_target_pairs={{4,0},{8,4},{12,8},{16,12},{20,16},{24,20},{28,24},{5,1},{9,5},{13... | collective-permute-start | bytes 147464 | tf_op jit(solution)/shard_map/ppermute | solution.py:30
  165.9 7.0 %collective-permute-start.13 = (f32[3,1,34,128]{3,2,1,0:T(8,128)S(1)}, f32[3,1,34,128]{3,2,1,0:T(8,128)S(1)}, u32[]{:S(2)}, u32[]{:S(2)}) collective-permute-start(f32[3,1,34,128]{3,2,1,0:T(8,128)S(1)} %get-tuple-element.46), channel_id=1, source_target_pairs={{1,0},{2,1},{3,2},{5,4},{6,5},{7,6},{9,8},{10,9},{11,10},{13,12},{... | collective-permute-start | bytes 156680 | tf_op jit(solution)/shard_map/ppermute | solution.py:30
  169.0 4.7 %collective-permute-start.14 = (f32[3,1,34,128]{3,2,1,0:T(8,128)S(1)}, f32[3,1,34,128]{3,2,1,0:T(8,128)S(1)}, u32[]{:S(2)}, u32[]{:S(2)}) collective-permute-start(f32[3,1,34,128]{3,2,1,0:T(8,128)S(1)} %get-tuple-element.47), channel_id=1, source_target_pairs={{0,1},{1,2},{2,3},{4,5},{5,6},{6,7},{8,9},{9,10},{10,11},{12,13},{... | collective-permute-start | bytes 156680 | tf_op jit(solution)/shard_map/ppermute | solution.py:29
  176.3 6.7 %collective-permute-start.15 = (f32[3,32,1,128]{3,2,1,0:T(1,128)S(1)}, f32[3,32,1,128]{3,2,1,0:T(1,128)S(1)}, u32[]{:S(2)}, u32[]{:S(2)}) collective-permute-start(f32[3,32,1,128]{3,2,1,0:T(1,128)S(1)} %get-tuple-element.65), channel_id=1, source_target_pairs={{0,4},{4,8},{8,12},{12,16},{16,20},{20,24},{24,28},{1,5},{5,9},{9,... | collective-permute-start | bytes 147464 | tf_op jit(solution)/shard_map/ppermute | solution.py:29
  178.4 5.7 %collective-permute-start.16 = (f32[3,32,1,128]{3,2,1,0:T(1,128)S(1)}, f32[3,32,1,128]{3,2,1,0:T(1,128)S(1)}, u32[]{:S(2)}, u32[]{:S(2)}) collective-permute-start(f32[3,32,1,128]{3,2,1,0:T(1,128)S(1)} %get-tuple-element.64), channel_id=1, source_target_pairs={{4,0},{8,4},{12,8},{16,12},{20,16},{24,20},{28,24},{5,1},{9,5},{13... | collective-permute-start | bytes 147464 | tf_op jit(solution)/shard_map/ppermute | solution.py:30
  184.2 8.1 %collective-permute-start.17 = (f32[3,1,34,128]{3,2,1,0:T(8,128)S(1)}, f32[3,1,34,128]{3,2,1,0:T(8,128)S(1)}, u32[]{:S(2)}, u32[]{:S(2)}) collective-permute-start(f32[3,1,34,128]{3,2,1,0:T(8,128)S(1)} %get-tuple-element.44), channel_id=1, source_target_pairs={{1,0},{2,1},{3,2},{5,4},{6,5},{7,6},{9,8},{10,9},{11,10},{13,12},{... | collective-permute-start | bytes 156680 | tf_op jit(solution)/shard_map/ppermute | solution.py:30
  186.1 6.7 %collective-permute-start.18 = (f32[3,1,34,128]{3,2,1,0:T(8,128)S(1)}, f32[3,1,34,128]{3,2,1,0:T(8,128)S(1)}, u32[]{:S(2)}, u32[]{:S(2)}) collective-permute-start(f32[3,1,34,128]{3,2,1,0:T(8,128)S(1)} %get-tuple-element.45), channel_id=1, source_target_pairs={{0,1},{1,2},{2,3},{4,5},{5,6},{6,7},{8,9},{9,10},{10,11},{12,13},{... | collective-permute-start | bytes 156680 | tf_op jit(solution)/shard_map/ppermute | solution.py:29
  192.8 9.1 %copy-start.21 = (f32[32,32,128]{2,1,0:T(8,128)S(1)}, f32[32,32,128]{2,1,0:T(8,128)}, u32[]{:S(2)}) copy-start(f32[32,32,128]{2,1,0:T(8,128)} %copy-done.20) | copy-start | bytes 1572868
  192.8 9.1 %copy-start.23 = (f32[32,32,128]{2,1,0:T(8,128)S(1)}, f32[32,32,128]{2,1,0:T(8,128)}, u32[]{:S(2)}) copy-start(f32[32,32,128]{2,1,0:T(8,128)} %copy-done.22) | copy-start | bytes 1572868
  192.8 9.2 %copy-start.25 = (f32[32,32,128]{2,1,0:T(8,128)S(1)}, f32[32,32,128]{2,1,0:T(8,128)}, u32[]{:S(2)}) copy-start(f32[32,32,128]{2,1,0:T(8,128)} %copy-done.24) | copy-start | bytes 1572868
  192.8 9.2 %copy-start.27 = (f32[32,32,128]{2,1,0:T(8,128)S(1)}, f32[32,32,128]{2,1,0:T(8,128)}, u32[]{:S(2)}) copy-start(f32[32,32,128]{2,1,0:T(8,128)} %copy-done.26) | copy-start | bytes 1572868
  192.8 9.2 %copy-start.29 = (f32[32,32,128]{2,1,0:T(8,128)S(1)}, f32[32,32,128]{2,1,0:T(8,128)}, u32[]{:S(2)}) copy-start(f32[32,32,128]{2,1,0:T(8,128)} %copy-done.28) | copy-start | bytes 1572868
  195.5 6.9 %collective-permute-start.19 = (f32[3,32,1,128]{3,2,1,0:T(1,128)S(1)}, f32[3,32,1,128]{3,2,1,0:T(1,128)S(1)}, u32[]{:S(2)}, u32[]{:S(2)}) collective-permute-start(f32[3,32,1,128]{3,2,1,0:T(1,128)S(1)} %get-tuple-element.61), channel_id=1, source_target_pairs={{0,4},{4,8},{8,12},{12,16},{16,20},{20,24},{24,28},{1,5},{5,9},{9,... | collective-permute-start | bytes 147464 | tf_op jit(solution)/shard_map/ppermute | solution.py:29
  200.0 4.8 %collective-permute-start.20 = (f32[3,32,1,128]{3,2,1,0:T(1,128)S(1)}, f32[3,32,1,128]{3,2,1,0:T(1,128)S(1)}, u32[]{:S(2)}, u32[]{:S(2)}) collective-permute-start(f32[3,32,1,128]{3,2,1,0:T(1,128)S(1)} %get-tuple-element.60), channel_id=1, source_target_pairs={{4,0},{8,4},{12,8},{16,12},{20,16},{24,20},{28,24},{5,1},{9,5},{13... | collective-permute-start | bytes 147464 | tf_op jit(solution)/shard_map/ppermute | solution.py:30
  202.3 10.7 %copy-start.36 = (f32[37,32,128]{2,1,0:T(8,128)}, f32[37,32,128]{2,1,0:T(8,128)S(1)}, u32[]{:S(2)}) copy-start(f32[37,32,128]{2,1,0:T(8,128)S(1)} %pad_add_fusion) | copy-start | bytes 1818628
  204.9 8.2 %collective-permute-start.21 = (f32[3,1,34,128]{3,2,1,0:T(8,128)S(1)}, f32[3,1,34,128]{3,2,1,0:T(8,128)S(1)}, u32[]{:S(2)}, u32[]{:S(2)}) collective-permute-start(f32[3,1,34,128]{3,2,1,0:T(8,128)S(1)} %get-tuple-element.42), channel_id=1, source_target_pairs={{1,0},{2,1},{3,2},{5,4},{6,5},{7,6},{9,8},{10,9},{11,10},{13,12},{... | collective-permute-start | bytes 156680 | tf_op jit(solution)/shard_map/ppermute | solution.py:30
  206.8 7.0 %collective-permute-start.22 = (f32[3,1,34,128]{3,2,1,0:T(8,128)S(1)}, f32[3,1,34,128]{3,2,1,0:T(8,128)S(1)}, u32[]{:S(2)}, u32[]{:S(2)}) collective-permute-start(f32[3,1,34,128]{3,2,1,0:T(8,128)S(1)} %get-tuple-element.43), channel_id=1, source_target_pairs={{0,1},{1,2},{2,3},{4,5},{5,6},{6,7},{8,9},{9,10},{10,11},{12,13},{... | collective-permute-start | bytes 156680 | tf_op jit(solution)/shard_map/ppermute | solution.py:29
  216.4 6.2 %collective-permute-start.23 = (f32[3,32,1,128]{3,2,1,0:T(1,128)S(1)}, f32[3,32,1,128]{3,2,1,0:T(1,128)S(1)}, u32[]{:S(2)}, u32[]{:S(2)}) collective-permute-start(f32[3,32,1,128]{3,2,1,0:T(1,128)S(1)} %get-tuple-element.57), channel_id=1, source_target_pairs={{0,4},{4,8},{8,12},{12,16},{16,20},{20,24},{24,28},{1,5},{5,9},{9,... | collective-permute-start | bytes 147464 | tf_op jit(solution)/shard_map/ppermute | solution.py:29
  218.9 5.1 %collective-permute-start.24 = (f32[3,32,1,128]{3,2,1,0:T(1,128)S(1)}, f32[3,32,1,128]{3,2,1,0:T(1,128)S(1)}, u32[]{:S(2)}, u32[]{:S(2)}) collective-permute-start(f32[3,32,1,128]{3,2,1,0:T(1,128)S(1)} %get-tuple-element.56), channel_id=1, source_target_pairs={{4,0},{8,4},{12,8},{16,12},{20,16},{24,20},{28,24},{5,1},{9,5},{13... | collective-permute-start | bytes 147464 | tf_op jit(solution)/shard_map/ppermute | solution.py:30
  224.1 7.9 %collective-permute-start.25 = (f32[3,1,34,128]{3,2,1,0:T(8,128)S(1)}, f32[3,1,34,128]{3,2,1,0:T(8,128)S(1)}, u32[]{:S(2)}, u32[]{:S(2)}) collective-permute-start(f32[3,1,34,128]{3,2,1,0:T(8,128)S(1)} %get-tuple-element.40), channel_id=1, source_target_pairs={{1,0},{2,1},{3,2},{5,4},{6,5},{7,6},{9,8},{10,9},{11,10},{13,12},{... | collective-permute-start | bytes 156680 | tf_op jit(solution)/shard_map/ppermute | solution.py:30
  226.0 6.7 %collective-permute-start.26 = (f32[3,1,34,128]{3,2,1,0:T(8,128)S(1)}, f32[3,1,34,128]{3,2,1,0:T(8,128)S(1)}, u32[]{:S(2)}, u32[]{:S(2)}) collective-permute-start(f32[3,1,34,128]{3,2,1,0:T(8,128)S(1)} %get-tuple-element.41), channel_id=1, source_target_pairs={{0,1},{1,2},{2,3},{4,5},{5,6},{6,7},{8,9},{9,10},{10,11},{12,13},{... | collective-permute-start | bytes 156680 | tf_op jit(solution)/shard_map/ppermute | solution.py:29
  235.3 74.5 %collective-permute-start.27 = (f32[3,32,1,128]{3,2,1,0:T(1,128)S(1)}, f32[3,32,1,128]{3,2,1,0:T(1,128)S(1)}, u32[]{:S(2)}, u32[]{:S(2)}) collective-permute-start(f32[3,32,1,128]{3,2,1,0:T(1,128)S(1)} %get-tuple-element.53), channel_id=1, source_target_pairs={{0,4},{4,8},{8,12},{12,16},{16,20},{20,24},{24,28},{1,5},{5,9},{9,... | collective-permute-start | bytes 147464 | tf_op jit(solution)/shard_map/ppermute | solution.py:29
  239.8 70.0 %collective-permute-start.28 = (f32[3,32,1,128]{3,2,1,0:T(1,128)S(1)}, f32[3,32,1,128]{3,2,1,0:T(1,128)S(1)}, u32[]{:S(2)}, u32[]{:S(2)}) collective-permute-start(f32[3,32,1,128]{3,2,1,0:T(1,128)S(1)} %get-tuple-element.52), channel_id=1, source_target_pairs={{4,0},{8,4},{12,8},{16,12},{20,16},{24,20},{28,24},{5,1},{9,5},{13... | collective-permute-start | bytes 147464 | tf_op jit(solution)/shard_map/ppermute | solution.py:30
  309.9 7.2 %collective-permute-start.29 = (f32[3,1,34,128]{3,2,1,0:T(8,128)S(1)}, f32[3,1,34,128]{3,2,1,0:T(8,128)S(1)}, u32[]{:S(2)}, u32[]{:S(2)}) collective-permute-start(f32[3,1,34,128]{3,2,1,0:T(8,128)S(1)} %get-tuple-element.38), channel_id=1, source_target_pairs={{1,0},{2,1},{3,2},{5,4},{6,5},{7,6},{9,8},{10,9},{11,10},{13,12},{... | collective-permute-start | bytes 156680 | tf_op jit(solution)/shard_map/ppermute | solution.py:30
  311.8 6.0 %collective-permute-start.30 = (f32[3,1,34,128]{3,2,1,0:T(8,128)S(1)}, f32[3,1,34,128]{3,2,1,0:T(8,128)S(1)}, u32[]{:S(2)}, u32[]{:S(2)}) collective-permute-start(f32[3,1,34,128]{3,2,1,0:T(8,128)S(1)} %get-tuple-element.39), channel_id=1, source_target_pairs={{0,1},{1,2},{2,3},{4,5},{5,6},{6,7},{8,9},{9,10},{10,11},{12,13},{... | collective-permute-start | bytes 156680 | tf_op jit(solution)/shard_map/ppermute | solution.py:29
  (29 other events, 150.0 us)
where the time goes:
time: 324 us; the launch traced here: 321 us
  local copies, waits for them, and re-layouts  107 us (33%)
  starting transfers between devices  105 us (32%)
  other arithmetic  92.9 us (29%)
  waiting for transfers between devices  8.25 us (3%)
  blocking collectives  5.1 us (2%)
    gather x1, local copies, waits for them, and re-layouts, local(): picked = jnp.take(momentum_cot.reshape(3, -1), band_index, axis=1)  59.8 us
    ppermute x15, starting transfers between devices, extended(): before = lax.ppermute(last, axis, up)  58.1 us
    ppermute x16, starting transfers between devices, extended(): after = lax.ppermute(initial, axis, down)  41.2 us
    unnamed x89, local copies, waits for them, and re-layouts  35.4 us
    scatter-add x1, other arithmetic, local(): level_flat = level_flat.at[band_index].add(-2.0 * strength)  22.6 us
    scatter-add x1, other arithmetic, local(): level_flat = level_flat.at[band_index - 1].add(strength)  22.6 us
    scatter-add x1, other arithmetic, local(): level_flat = level_flat.at[band_index + 1].add(strength)  22.6 us
    add x6, other arithmetic, local(): momentum = momentum + rate_value * diffuse(padded_field, padded_mu)  16.1 us
  transfers between devices with their start and end apart: 33, of which 8 were waited for; matrix products, arithmetic and copies ran while one was open for 60% of the time, Pallas kernels for 0%

commit v1 on v0

v1 whole, which is shorter than its diff:
```python
import functools
import math

import jax
import jax.numpy as jnp
from jax import lax
from jax.experimental import pallas as pl
from jax.experimental.pallas import tpu as pltpu
from jax.sharding import PartitionSpec as P

MESH = pl.DeviceIdType.MESH
RATE = 0.05
W1 = 4
W2 = 2
CHUNK = 512
FACES = 3


def kernel(
    n_row,
    n_col,
    cot_hbm,
    state_hbm,
    mom_hbm,
    courant_hbm,
    stencil_hbm,
    upwind_hbm,
    visc_hbm,
    cells_ref,
    count_ref,
    force_ref,
    basis_ref,
    level_out,
    mom_out,
    grad_out,
    field,
    other,
    coef,
    lev,
    codes,
    band_sum,
    product,
    pack_lo,
    pack_hi,
    got_lo,
    got_hi,
    pack2_lo,
    pack2_hi,
    got2_lo,
    got2_hi,
    side2_lo,
    side2_hi,
    mine,
    partials,
    local_sem,
    send_sem,
    recv_sem,
    part_send,
    part_recv,
):
    nx, ny, nz = cot_hbm.shape
    row = lax.axis_index("row")
    col = lax.axis_index("col")
    has = {
        ("row", -1): row > 0,
        ("row", 1): row < n_row - 1,
        ("col", -1): col > 0,
        ("col", 1): col < n_col - 1,
    }

    def exists(dr, dc):
        cond = None
        for axis, d in (("row", dr), ("col", dc)):
            if d:
                here = has[(axis, d)]
                cond = here if cond is None else jnp.logical_and(cond, here)
        return cond

    barrier = pltpu.get_barrier_semaphore()
    expected = jnp.int32(n_col - 1)
    for d in range(1, n_col):
        pl.semaphore_signal(
            barrier, inc=1, device_id=(row, lax.rem(col + d, n_col)), device_id_type=MESH
        )
    for dr in (-1, 1):
        for dc in (-1, 0, 1):
            cond = exists(dr, dc)

            @pl.when(cond)
            def _(dr=dr, dc=dc):
                pl.semaphore_signal(
                    barrier, inc=1, device_id=(row + dr, col + dc), device_id_type=MESH
                )

            expected = expected + jnp.where(cond, 1, 0).astype(jnp.int32)

    local = []

    def fetch(src, dst):
        copy = pltpu.make_async_copy(src, dst, local_sem.at[len(local)])
        copy.start()
        local.append(copy)

    for k in range(3):
        fetch(mom_hbm.at[k], field.at[k, W1 : W1 + nx, 0:ny])
    fetch(visc_hbm, field.at[3, W1 : W1 + nx, 0:ny])
    for slot, src in enumerate((cot_hbm, state_hbm, courant_hbm)):
        fetch(src, lev.at[slot, FACES : FACES + nx])
    for slot, src in enumerate((stencil_hbm, upwind_hbm)):
        fetch(src, codes.at[slot, FACES : FACES + nx])

    sends = []

    def remote(src, dst, dr, dc):
        i = len(sends)
        copy = pltpu.make_async_remote_copy(
            src_ref=src,
            dst_ref=dst,
            send_sem=send_sem.at[i],
            recv_sem=recv_sem.at[i],
            device_id=(row + dr, col + dc),
            device_id_type=MESH,
        )

        @pl.when(exists(dr, dc))
        def _():
            copy.start()

        sends.append((copy, dr, dc))
        return sends[-1]

    def arrived(entry):
        copy, dr, dc = entry

        @pl.when(exists(-dr, -dc))
        def _():
            copy.wait_recv()

    def departed(entry):
        copy, dr, dc = entry

        @pl.when(exists(dr, dc))
        def _():
            copy.wait_send()

    for copy in local[:4]:
        copy.wait()

    def pack(x, _):
        for k in range(4):
            pack_lo[k, x] = field[k, W1 + x, 0:8][0:W1]
            pack_hi[k, x] = field[k, W1 + x, ny - 8 : ny][8 - W1 : 8]
        return 0

    lax.fori_loop(0, nx, pack, 0)
    pl.semaphore_wait(barrier, expected)

    first = [
        remote(pack_hi, got_lo.at[:, W1 : W1 + nx], 1, 0),
        remote(pack_lo, got_hi.at[:, W1 : W1 + nx], -1, 0),
        remote(pack_hi.at[:, nx - W1 : nx], got_lo.at[:, 0:W1], 1, 1),
        remote(pack_hi.at[:, 0:W1], got_lo.at[:, W1 + nx : 2 * W1 + nx], 1, -1),
        remote(pack_lo.at[:, nx - W1 : nx], got_hi.at[:, 0:W1], -1, 1),
        remote(pack_lo.at[:, 0:W1], got_hi.at[:, W1 + nx : 2 * W1 + nx], -1, -1),
    ]
    for copy in local[4:]:
        copy.wait()
    level_sends = [
        remote(lev.at[:, nx : nx + FACES], lev.at[:, 0:FACES], 0, 1),
        remote(codes.at[:, nx : nx + FACES], codes.at[:, 0:FACES], 0, 1),
        remote(lev.at[:, FACES : 2 * FACES], lev.at[:, nx + FACES : nx + 2 * FACES], 0, -1),
        remote(codes.at[:, FACES : 2 * FACES], codes.at[:, nx + FACES : nx + 2 * FACES], 0, -1),
    ]
    first += [
        remote(field.at[:, nx : nx + W1, 0:ny], field.at[:, 0:W1, 0:ny], 0, 1),
        remote(
            field.at[:, W1 : 2 * W1, 0:ny], field.at[:, nx + W1 : nx + 2 * W1, 0:ny], 0, -1
        ),
    ]

    count = count_ref[0, 0]
    band_cap = cells_ref.shape[-1]

    def band(step, _):
        at = pl.multiple_of(step * CHUNK, CHUNK)
        cell = cells_ref[0, :, pl.ds(at, CHUNK)]
        entry = at + lax.broadcasted_iota(jnp.int32, (1, CHUNK), 1)
        line = cell // nz
        z = cell - line * nz
        lines = lax.broadcasted_iota(jnp.int32, (nx * ny, CHUNK), 0) == line
        left = jnp.where(lines, 1.0, 0.0).astype(jnp.bfloat16)
        hit = lax.broadcasted_iota(jnp.int32, (nz, CHUNK), 0) == z
        parts = []
        for k in range(3):
            force = jnp.where(entry < count, force_ref[k, 0, :, pl.ds(at, CHUNK)], 0.0)
            high = force.astype(jnp.bfloat16).astype(jnp.float32)
            for part in (high, force - high):
                parts.append(jnp.where(hit, part, 0.0).astype(jnp.bfloat16))
        right = jnp.concatenate(parts, axis=0)
        total = lax.dot_general(
            left, right, (((1,), (1,)), ((), ())), preferred_element_type=jnp.float32
        )

        @pl.when(step == 0)
        def _():
            band_sum[...] = total

        @pl.when(step > 0)
        def _():
            band_sum[...] += total

        return 0

    lax.fori_loop(0, band_cap // CHUNK, band, 0)

    for entry in level_sends:
        arrived(entry)

    @pl.when(jnp.logical_not(has[("col", -1)]))
    def _():
        lev[:, 0:FACES] = jnp.zeros((3, FACES, ny, nz), jnp.float32)
        codes[:, 0:FACES] = jnp.zeros((2, FACES, ny, nz), jnp.int32)

    @pl.when(jnp.logical_not(has[("col", 1)]))
    def _():
        lev[:, nx + FACES : nx + 2 * FACES] = jnp.zeros((3, FACES, ny, nz), jnp.float32)
        codes[:, nx + FACES : nx + 2 * FACES] = jnp.zeros((2, FACES, ny, nz), jnp.int32)

    def face(e, carry, with_product, with_out):
        up = codes[1, e]
        sten = codes[0, e]
        below = up == 0
        is_a = jnp.logical_and(below, sten == 0)
        is_d = jnp.logical_and(jnp.logical_not(below), sten == 0)
        is_b = sten == jnp.where(below, 1, 2)
        g = col * nx + e - FACES
        inside = jnp.logical_and(g >= 0, g < n_col * nx - 1)
        speed = lev[2, e] * jnp.where(below, 1.0, -1.0)
        speed = jnp.where(inside, speed, 0.0)
        weighted = (lev[0, e + 1] - lev[0, e]) * speed
        zero = 0.0
        wts = (
            jnp.where(is_a, 1 / 3, zero),
            jnp.where(is_a, -7 / 6, jnp.where(is_b, -1 / 6, zero)),
            jnp.where(is_a, 11 / 6, jnp.where(is_b, 5 / 6, jnp.where(is_d, zero, 1 / 3))),
            jnp.where(is_d, 11 / 6, jnp.where(is_b, 1 / 3, jnp.where(is_a, zero, 5 / 6))),
            jnp.where(is_d, -7 / 6, jnp.where(jnp.logical_or(is_a, is_b), zero, -1 / 6)),
            jnp.where(is_d, 1 / 3, zero),
        )
        sums = [c + weighted * w for c, w in zip(carry, wts)]
        if with_product:
            value = wts[0] * lev[1, e - 2]
            for m in range(1, 6):
                value = value + wts[m] * lev[1, e - 2 + m]
            at = pl.multiple_of((e - FACES) * ny, ny)
            product[pl.ds(at, ny), :] = weighted * value
        if with_out:
            j = e - 5
            at = pl.multiple_of(j * ny, ny)
            strength = jnp.zeros((ny, nz), jnp.float32)
            for k in range(3):
                force = (
                    band_sum[pl.ds(at, ny), 2 * k * nz : (2 * k + 1) * nz]
                    + band_sum[pl.ds(at, ny), (2 * k + 1) * nz : (2 * k + 2) * nz]
                )
                strength = strength + force * field[k, W1 + j, 0:ny]
            bend = pltpu.roll(strength, 1, 1) + pltpu.roll(strength, nz - 1, 1) - 2.0 * strength
            level_out[j] = lev[0, j + FACES] + sums[0] + bend
        return tuple(sums[1:]) + (jnp.zeros((ny, nz), jnp.float32),)

    carry = tuple(jnp.zeros((ny, nz), jnp.float32) for _ in range(6))
    for low, high, with_product, with_out in (
        (0, 3, False, False),
        (3, 5, True, False),
        (5, nx + 3, True, True),
        (nx + 3, nx + 5, False, True),
    ):
        carry = lax.fori_loop(
            low,
            high,
            functools.partial(face, with_product=with_product, with_out=with_out),
            carry,
        )
    mine[...] = jnp.dot(
        basis_ref[...],
        product[...],
        precision=lax.Precision.HIGHEST,
        preferred_element_type=jnp.float32,
    )
    part_copies = []
    for d in range(1, n_col):
        copy = pltpu.make_async_remote_copy(
            src_ref=mine,
            dst_ref=partials.at[d],
            send_sem=part_send.at[d],
            recv_sem=part_recv.at[d],
            device_id=(row, lax.rem(col + d, n_col)),
            device_id_type=MESH,
        )
        copy.start()
        part_copies.append(copy)

    for entry in first:
        arrived(entry)

    def line_of(x, width, lo_ref, hi_ref, k):
        left = x < width
        right = x >= width + nx
        in_col = jnp.logical_and(
            jnp.logical_or(jnp.logical_not(left), has[("col", -1)]),
            jnp.logical_or(jnp.logical_not(right), has[("col", 1)]),
        )
        hi = jnp.where(jnp.logical_and(in_col, has[("row", 1)]), hi_ref[k, x], 0.0)
        lo = jnp.where(jnp.logical_and(in_col, has[("row", -1)]), lo_ref[k, x], 0.0)
        return hi, lo

    def unpack(x, _):
        for k in range(4):
            hi, lo = line_of(x, W1, got_lo, got_hi, k)
            field[k, x, ny : ny + 8] = jnp.concatenate([hi, lo], axis=0)
        return 0

    lax.fori_loop(0, nx + 2 * W1, unpack, 0)

    @pl.when(jnp.logical_not(has[("col", -1)]))
    def _():
        field[:, 0:W1, 0:ny] = jnp.zeros((4, W1, ny, nz), jnp.float32)

    @pl.when(jnp.logical_not(has[("col", 1)]))
    def _():
        field[:, nx + W1 : nx + 2 * W1, 0:ny] = jnp.zeros((4, W1, ny, nz), jnp.float32)

    tall = ny + 8
    sub = lax.broadcasted_iota(jnp.int32, (tall, nz), 0)
    lane = lax.broadcasted_iota(jnp.int32, (tall, nz), 1)
    up_there = jnp.where(has[("row", 1)], 1, 0)
    down_there = jnp.where(has[("row", -1)], 1, 0)
    y_inside = jnp.where(sub < ny, 1, jnp.where(sub < ny + 4, up_there, down_there)) > 0

    def coefficients(x, _):
        left = jnp.where(x < W1, jnp.where(has[("col", -1)], 1, 0), 1)
        right = jnp.where(x >= W1 + nx, jnp.where(has[("col", 1)], 1, 0), 1)
        inside = jnp.logical_and(y_inside, left * right > 0)
        mu = field[3, x]
        half = 0.5 * RATE
        near = [
            half * (mu + field[3, x + 1]),
            half * (mu + field[3, x - 1]),
            half * (mu + pltpu.roll(mu, tall - 1, 0)),
            half * (mu + pltpu.roll(mu, 1, 0)),
            half * (mu + jnp.where(lane == nz - 1, 0.0, pltpu.roll(mu, nz - 1, 1))),
            half * (mu + jnp.where(lane == 0, 0.0, pltpu.roll(mu, 1, 1))),
        ]
        own = 1.0 - (((near[0] + near[1]) + (near[2] + near[3])) + (near[4] + near[5]))
        near[4] = jnp.where(lane == nz - 1, 0.0, near[4])
        near[5] = jnp.where(lane == 0, 0.0, near[5])
        for slot, value in enumerate([own] + near):
            coef[slot, x] = jnp.where(inside, value, 0.0)
        return 0

    lax.fori_loop(1, nx + 2 * W1 - 1, coefficients, 0)

    def advance(src, dst, low, high, last):
        def one(x, _):
            for k in range(3):
                v = src[k, x]
                new = (
                    coef[0, x] * v
                    + coef[1, x] * src[k, x + 1]
                    + coef[2, x] * src[k, x - 1]
                    + coef[3, x] * pltpu.roll(v, tall - 1, 0)
                    + coef[4, x] * pltpu.roll(v, 1, 0)
                    + coef[5, x] * pltpu.roll(v, nz - 1, 1)
                    + coef[6, x] * pltpu.roll(v, 1, 1)
                )
                if last:
                    dst[k, x - W1] = new[0:ny]
                else:
                    dst[k, x] = new
            return 0

        lax.fori_loop(low, high, one, 0)

    end = nx + 2 * W1
    advance(field, other, 1, end - 1, False)
    for entry in first[-2:]:
        departed(entry)
    advance(other, field, 2, end - 2, False)
    advance(field, other, 3, end - 3, False)
    advance(other, field, 4, end - 4, False)

    def pack2(x, _):
        for k in range(3):
            pack2_lo[k, x] = field[k, W1 + x, 0:8][0:W2]
            pack2_hi[k, x] = field[k, W1 + x, ny - 8 : ny][8 - W2 : 8]
        return 0

    lax.fori_loop(0, nx, pack2, 0)
    second = [
        remote(pack2_hi, got2_lo.at[:, W2 : W2 + nx], 1, 0),
        remote(pack2_lo, got2_hi.at[:, W2 : W2 + nx], -1, 0),
        remote(pack2_hi.at[:, nx - W2 : nx], got2_lo.at[:, 0:W2], 1, 1),
        remote(pack2_hi.at[:, 0:W2], got2_lo.at[:, W2 + nx : 2 * W2 + nx], 1, -1),
        remote(pack2_lo.at[:, nx - W2 : nx], got2_hi.at[:, 0:W2], -1, 1),
        remote(pack2_lo.at[:, 0:W2], got2_hi.at[:, W2 + nx : 2 * W2 + nx], -1, -1),
        remote(field.at[0:3, W1 + nx - W2 : W1 + nx, 0:ny], side2_lo, 0, 1),
        remote(field.at[0:3, W1 : W1 + W2, 0:ny], side2_hi, 0, -1),
    ]

    total = mine[...]
    for d, copy in zip(range(1, n_col), part_copies):
        copy.wait_recv()
        total = total + partials[d]
    summed = lax.dot_general(
        jnp.ones((8, nz), jnp.float32),
        total,
        (((1,), (1,)), ((), ())),
        precision=lax.Precision.HIGHEST,
        preferred_element_type=jnp.float32,
    )
    grad_out[...] = summed[0:1] / math.sqrt(n_col * nx * ny * nz)

    for entry in second:
        arrived(entry)
    gap = jnp.zeros((8 - 2 * W2, nz), jnp.float32)

    def unpack2(x, _):
        for k in range(3):
            hi, lo = line_of(x, W2, got2_lo, got2_hi, k)
            field[k, x + W1 - W2, ny : ny + 8] = jnp.concatenate([hi, gap, lo], axis=0)
        return 0

    lax.fori_loop(0, nx + 2 * W2, unpack2, 0)
    for k in range(3):
        field[k, W1 - W2 : W1, 0:ny] = jnp.where(has[("col", -1)], side2_lo[k], 0.0)
        field[k, W1 + nx : W1 + nx + W2, 0:ny] = jnp.where(has[("col", 1)], side2_hi[k], 0.0)
    advance(field, other, W1 - 1, W1 + nx + 1, False)
    advance(other, mom_out, W1, W1 + nx, True)

    for entry in first[:-2] + level_sends + second:
        departed(entry)
    for copy in part_copies:
        copy.wait_send()


def local(
    n_row,
    n_col,
    level_cot,
    level_state,
    momentum_cot,
    courant,
    stencil,
    upwind,
    viscosity,
    band_cells,
    band_count,
    band_force,
    design_basis,
):
    nx, ny, nz = level_cot.shape
    ndes = design_basis.shape[0]
    basis = design_basis.reshape(ndes, nx * ny)
    wide, tall = nx + 2 * W1, ny + 8
    f32 = jnp.float32
    anywhere = pl.BlockSpec(memory_space=pl.ANY)
    vmem = pl.BlockSpec(memory_space=pltpu.VMEM)
    smem = pl.BlockSpec(memory_space=pltpu.SMEM)
    return pl.pallas_call(
        functools.partial(kernel, n_row, n_col),
        out_shape=(
            jax.ShapeDtypeStruct((nx, ny, nz), f32),
            jax.ShapeDtypeStruct((3, nx, ny, nz), f32),
            jax.ShapeDtypeStruct((1, ndes), f32),
        ),
        in_specs=[anywhere] * 7 + [vmem, smem, vmem, vmem],
        out_specs=(vmem, vmem, vmem),
        scratch_shapes=[
            pltpu.VMEM((4, wide, tall, nz), f32),
            pltpu.VMEM((3, wide, tall, nz), f32),
            pltpu.VMEM((7, wide, tall, nz), f32),
            pltpu.VMEM((3, nx + 2 * FACES, ny, nz), f32),
            pltpu.VMEM((2, nx + 2 * FACES, ny, nz), jnp.int32),
            pltpu.VMEM((nx * ny, 6 * nz), f32),
            pltpu.VMEM((nx * ny, nz), f32),
            pltpu.VMEM((4, nx, W1, nz), f32),
            pltpu.VMEM((4, nx, W1, nz), f32),
            pltpu.VMEM((4, wide, W1, nz), f32),
            pltpu.VMEM((4, wide, W1, nz), f32),
            pltpu.VMEM((3, nx, W2, nz), f32),
            pltpu.VMEM((3, nx, W2, nz), f32),
            pltpu.VMEM((3, nx + 2 * W2, W2, nz), f32),
            pltpu.VMEM((3, nx + 2 * W2, W2, nz), f32),
            pltpu.VMEM((3, W2, ny, nz), f32),
            pltpu.VMEM((3, W2, ny, nz), f32),
            pltpu.VMEM((ndes, nz), f32),
            pltpu.VMEM((n_col, ndes, nz), f32),
            pltpu.SemaphoreType.DMA((9,)),
            pltpu.SemaphoreType.DMA((20,)),
            pltpu.SemaphoreType.DMA((20,)),
            pltpu.SemaphoreType.DMA((n_col,)),
            pltpu.SemaphoreType.DMA((n_col,)),
        ],
        compiler_params=pltpu.CompilerParams(
            collective_id=0, has_side_effects=True, vmem_limit_bytes=50 * 1024 * 1024
        ),
    )(
        level_cot,
        level_state,
        momentum_cot,
        courant,
        stencil,
        upwind,
        viscosity,
        band_cells,
        band_count,
        band_force,
        basis,
    )


def solution(mesh):
    placed = (
        P("col", "row", None),
        P("col", "row", None),
        P(None, "col", "row", None),
        P("col", "row", None),
        P("col", "row", None),
        P("col", "row", None),
        P("col", "row", None),
        P("col", "row", None),
        P("col", "row"),
        P(None, "col", "row", None),
        P(None, "col", "row"),
    )
    return jax.shard_map(
        functools.partial(local, mesh.shape["row"], mesh.shape["col"]),
        mesh=mesh,
        in_specs=placed,
        out_specs=(P("col", "row", None), P(None, "col", "row", None), P("row", None)),
        check_vma=False,
    )
```

time: 324 us -> 66.1 us (0.20)
  starting transfers between devices: 105 us -> 0 us
  local copies, waits for them, and re-layouts: 107 us -> 12.8 us
  other arithmetic: 92.9 us -> 0 us
  Pallas kernels: 0 us -> 51.3 us
  waiting for transfers between devices: 8.25 us -> 0 us
  blocking collectives: 5.1 us -> 0 us
    ppermute x33 -> x0, starting transfers between devices: 105 us -> none  [the longest x15 58.1 us: extended(): before = lax.ppermute(last, axis, up)]
    scatter-add x5 -> x0, other arithmetic: 67.9 us -> none  [the longest x1 22.6 us: local(): level_flat = level_flat.at[band_index].add(-2.0 * strength)]
    gather x1 -> x0, local copies, waits for them, and re-layouts: 59.8 us -> none  [local(): picked = jnp.take(momentum_cot.reshape(3, -1), band_index, axis=1)]
    pallas_call x0 -> x1, Pallas kernels: none -> 51.3 us  [local(): pl.pallas_call(functools.partial(kernel, n_row, n_col), out_shape=(jax.Sh...]
    unnamed x89 -> x19, local copies, waits for them, and re-layouts: 35.4 us -> 11.7 us
    add x8 -> x0, other arithmetic: 16.5 us -> none  [the longest x6 16.1 us: local(): momentum = momentum + rate_value * diffuse(padded_field, padded_mu)]
    slice x18 -> x0, local copies, waits for them, and re-layouts: 12 us -> none  [the longest x6 5.12 us: diffuse(): upper = jnp.pad(centre[..., 1:], ((0, 0), (0, 0), (0, 0), (0, 1)))]
    ppermute x33 -> x0, waiting for transfers between devices: 8.25 us -> none  [the longest x16 5.04 us: extended(): after = lax.ppermute(initial, axis, down)]
  transfers between devices with their start and end apart: 33 -> 0, of which waited for: 8 -> 0; matrix products, arithmetic and copies ran while one was open for 60% -> 0% of each run, Pallas kernels for 0% -> 0%
where the time goes in v1:
time: 66.1 us; the launch traced here: 65.4 us
  Pallas kernels  51.3 us (78%)
  local copies, waits for them, and re-layouts  12.8 us (19%)
  between operations  1.3 us (2%)
    pallas_call x1, Pallas kernels, local(): pl.pallas_call(functools.partial(kernel, n_row, n_col), out_shape=(jax.Sh...  51.3 us
    unnamed x19, local copies, waits for them, and re-layouts  11.7 us

profile of v1, /device:TPU:9, one launch (start us, length us, event | category | flops | bytes accessed | tf_op | source)
XLA Modules:
  0.0 65.4 jit_solution(3290007304342239788)
XLA Ops:
  1.3 1.1 %reshape.9.basis_ref = f32[16,1024]{1,0:T(8,128)S(1)} reshape(f32[16,32,32]{2,1,0:T(8,128)} %param.21) | data formatting | bytes 131072 | tf_op jit(solution)/shard_map/reshape | solution.py:463
  2.4 0.0 copy-start
  2.4 1.0 %copy-done = f32[32,32,128]{2,1,0:T(8,128)S(1)} copy-done((f32[32,32,128]{2,1,0:T(8,128)S(1)}, f32[32,32,128]{2,1,0:T(8,128)}, u32[]{:S(2)}) %copy-start) | copy-done | bytes 524312
  3.4 0.0 copy-start.1
  3.4 1.0 %copy-done.1 = f32[32,32,128]{2,1,0:T(8,128)S(1)} copy-done((f32[32,32,128]{2,1,0:T(8,128)S(1)}, f32[32,32,128]{2,1,0:T(8,128)}, u32[]{:S(2)}) %copy-start.1) | copy-done | bytes 524312
  4.5 0.0 copy-start.2
  4.5 1.0 %copy-done.2 = f32[32,32,128]{2,1,0:T(8,128)S(1)} copy-done((f32[32,32,128]{2,1,0:T(8,128)S(1)}, f32[32,32,128]{2,1,0:T(8,128)}, u32[]{:S(2)}) %copy-start.2) | copy-done | bytes 524312
  5.5 0.0 copy-start.3
  5.5 1.0 %copy-done.3 = s32[32,32,128]{2,1,0:T(8,128)S(1)} copy-done((s32[32,32,128]{2,1,0:T(8,128)S(1)}, s32[32,32,128]{2,1,0:T(8,128)}, u32[]{:S(2)}) %copy-start.3) | copy-done | bytes 524312
  6.5 0.0 copy-start.4
  6.5 1.0 %copy-done.4 = s32[32,32,128]{2,1,0:T(8,128)S(1)} copy-done((s32[32,32,128]{2,1,0:T(8,128)S(1)}, s32[32,32,128]{2,1,0:T(8,128)}, u32[]{:S(2)}) %copy-start.4) | copy-done | bytes 524312
  7.6 0.0 copy-start.5
  7.6 1.0 %copy-done.5 = f32[32,32,128]{2,1,0:T(8,128)S(1)} copy-done((f32[32,32,128]{2,1,0:T(8,128)S(1)}, f32[32,32,128]{2,1,0:T(8,128)}, u32[]{:S(2)}) %copy-start.5) | copy-done | bytes 524312
  8.6 0.0 copy-start.6
  8.6 0.8 %copy-done.6 = f32[3,1,1,4096]{3,2,1,0:T(1,128)S(1)} copy-done((f32[3,1,1,4096]{3,2,1,0:T(1,128)S(1)}, f32[3,1,1,4096]{3,2,1,0:T(1,128)}, u32[]{:S(2)}) %copy-start.6) | copy-done | bytes 49176
  9.4 0.0 copy-start.7
  9.4 0.7 %copy-done.7 = s32[1,1,4096]{2,1,0:T(1,128)S(1)} copy-done((s32[1,1,4096]{2,1,0:T(1,128)S(1)}, s32[1,1,4096]{2,1,0:T(1,128)}, u32[]{:S(2)}) %copy-start.7) | copy-done | bytes 16408
  10.1 51.3 %shard_map.130 = (f32[32,32,128]{2,1,0:T(8,128)S(1)}, f32[3,32,32,128]{3,2,1,0:T(8,128)}, f32[1,16]{1,0:T(1,128)S(1)}) custom-call(f32[32,32,128]{2,1,0:T(8,128)S(1)} %copy-done, f32[32,32,128]{2,1,0:T(8,128)S(1)} %copy-done.1, f32[3,32,32,128]{3,2,1,0:T(8,128)} %mom_hbm.1, f32[32,32,128]{2,1,0:T(8,128)S(1)} %copy-done.2, s32[32,32,128]{2,1,0:T(8,128)S(1)} %copy-done.3, ...), custom_call_target="tpu_custom_call" | custom-call | tf_op jit(solution)/shard_map/pallas_call | solution.py:469
  61.5 0.8 %copy.18 = f32[32,32,128]{2,1,0:T(8,128)} copy(f32[32,32,128]{2,1,0:T(8,128)S(1)} %get-tuple-element.6) | data formatting | bytes 1048576
  62.3 2.7 %copy.19 = f32[3,32,32,128]{3,2,1,0:T(8,128)} copy(f32[3,32,32,128]{3,2,1,0:T(8,128)} %get-tuple-element.7) | data formatting | bytes 3145728
  64.9 0.5 copy.20
Async XLA Ops:
  2.4 1.0 %copy-start = (f32[32,32,128]{2,1,0:T(8,128)S(1)}, f32[32,32,128]{2,1,0:T(8,128)}, u32[]{:S(2)}) copy-start(f32[32,32,128]{2,1,0:T(8,128)} %cot_hbm.1) | copy-start | bytes 1572868
  3.4 1.0 %copy-start.1 = (f32[32,32,128]{2,1,0:T(8,128)S(1)}, f32[32,32,128]{2,1,0:T(8,128)}, u32[]{:S(2)}) copy-start(f32[32,32,128]{2,1,0:T(8,128)} %state_hbm.1) | copy-start | bytes 1572868
  4.5 1.0 %copy-start.2 = (f32[32,32,128]{2,1,0:T(8,128)S(1)}, f32[32,32,128]{2,1,0:T(8,128)}, u32[]{:S(2)}) copy-start(f32[32,32,128]{2,1,0:T(8,128)} %courant_hbm.1) | copy-start | bytes 1572868
  5.5 1.0 %copy-start.3 = (s32[32,32,128]{2,1,0:T(8,128)S(1)}, s32[32,32,128]{2,1,0:T(8,128)}, u32[]{:S(2)}) copy-start(s32[32,32,128]{2,1,0:T(8,128)} %stencil_hbm.1) | copy-start | bytes 1572868
  6.5 1.0 %copy-start.4 = (s32[32,32,128]{2,1,0:T(8,128)S(1)}, s32[32,32,128]{2,1,0:T(8,128)}, u32[]{:S(2)}) copy-start(s32[32,32,128]{2,1,0:T(8,128)} %upwind_hbm.1) | copy-start | bytes 1572868
  7.6 1.0 %copy-start.5 = (f32[32,32,128]{2,1,0:T(8,128)S(1)}, f32[32,32,128]{2,1,0:T(8,128)}, u32[]{:S(2)}) copy-start(f32[32,32,128]{2,1,0:T(8,128)} %visc_hbm.1) | copy-start | bytes 1572868
  8.6 0.8 %copy-start.6 = (f32[3,1,1,4096]{3,2,1,0:T(1,128)S(1)}, f32[3,1,1,4096]{3,2,1,0:T(1,128)}, u32[]{:S(2)}) copy-start(f32[3,1,1,4096]{3,2,1,0:T(1,128)} %force_ref.1) | copy-start | bytes 147460
  9.4 0.7 %copy-start.7 = (s32[1,1,4096]{2,1,0:T(1,128)S(1)}, s32[1,1,4096]{2,1,0:T(1,128)}, u32[]{:S(2)}) copy-start(s32[1,1,4096]{2,1,0:T(1,128)} %cells_ref.1) | copy-start | bytes 49156

commit v2 on v1

--- a/solution.py
+++ b/solution.py
@@ -26,10 +26,10 @@
     stencil_hbm,
     upwind_hbm,
     visc_hbm,
-    cells_ref,
+    cells_hbm,
     count_ref,
-    force_ref,
-    basis_ref,
+    force_hbm,
+    basis_hbm,
     level_out,
     mom_out,
     grad_out,
@@ -52,6 +52,10 @@
     side2_hi,
     mine,
     partials,
+    cells_ref,
+    force_ref,
+    basis_ref,
+    basis_flat,
     local_sem,
     send_sem,
     recv_sem,
@@ -108,6 +112,9 @@
         fetch(src, lev.at[slot, FACES : FACES + nx])
     for slot, src in enumerate((stencil_hbm, upwind_hbm)):
         fetch(src, codes.at[slot, FACES : FACES + nx])
+    fetch(cells_hbm, cells_ref)
+    fetch(force_hbm, force_ref)
+    fetch(basis_hbm, basis_ref)
 
     sends = []
 
@@ -152,17 +159,29 @@
             pack_hi[k, x] = field[k, W1 + x, ny - 8 : ny][8 - W1 : 8]
         return 0
 
-    lax.fori_loop(0, nx, pack, 0)
+    lax.fori_loop(0, nx, pack, 0, unroll=4)
     pl.semaphore_wait(barrier, expected)
 
-    first = [
-        remote(pack_hi, got_lo.at[:, W1 : W1 + nx], 1, 0),
-        remote(pack_lo, got_hi.at[:, W1 : W1 + nx], -1, 0),
-        remote(pack_hi.at[:, nx - W1 : nx], got_lo.at[:, 0:W1], 1, 1),
-        remote(pack_hi.at[:, 0:W1], got_lo.at[:, W1 + nx : 2 * W1 + nx], 1, -1),
-        remote(pack_lo.at[:, nx - W1 : nx], got_hi.at[:, 0:W1], -1, 1),
-        remote(pack_lo.at[:, 0:W1], got_hi.at[:, W1 + nx : 2 * W1 + nx], -1, -1),
-    ]
+    def line_sends(c):
+        return [
+            remote(pack_hi.at[c], got_lo.at[c, W1 : W1 + nx], 1, 0),
+            remote(pack_lo.at[c], got_hi.at[c, W1 : W1 + nx], -1, 0),
+            remote(pack_hi.at[c, nx - W1 : nx], got_lo.at[c, 0:W1], 1, 1),
+            remote(pack_hi.at[c, 0:W1], got_lo.at[c, W1 + nx : 2 * W1 + nx], 1, -1),
+            remote(pack_lo.at[c, nx - W1 : nx], got_hi.at[c, 0:W1], -1, 1),
+            remote(pack_lo.at[c, 0:W1], got_hi.at[c, W1 + nx : 2 * W1 + nx], -1, -1),
+        ]
+
+    def plane_sends(c):
+        return [
+            remote(field.at[c, nx : nx + W1, 0:ny], field.at[c, 0:W1, 0:ny], 0, 1),
+            remote(
+                field.at[c, W1 : 2 * W1, 0:ny], field.at[c, nx + W1 : nx + 2 * W1, 0:ny], 0, -1
+            ),
+        ]
+
+    mu_sends = line_sends(slice(3, 4))
+    first = line_sends(slice(0, 3))
     for copy in local[4:]:
         copy.wait()
     level_sends = [
@@ -171,12 +190,8 @@
         remote(lev.at[:, FACES : 2 * FACES], lev.at[:, nx + FACES : nx + 2 * FACES], 0, -1),
         remote(codes.at[:, FACES : 2 * FACES], codes.at[:, nx + FACES : nx + 2 * FACES], 0, -1),
     ]
-    first += [
-        remote(field.at[:, nx : nx + W1, 0:ny], field.at[:, 0:W1, 0:ny], 0, 1),
-        remote(
-            field.at[:, W1 : 2 * W1, 0:ny], field.at[:, nx + W1 : nx + 2 * W1, 0:ny], 0, -1
-        ),
-    ]
+    mu_sends += plane_sends(slice(3, 4))
+    first += plane_sends(slice(0, 3))
 
     count = count_ref[0, 0]
     band_cap = cells_ref.shape[-1]
@@ -212,6 +227,12 @@
         return 0
 
     lax.fori_loop(0, band_cap // CHUNK, band, 0)
+
+    group = nz // ny
+    for q in range(nx // group):
+        basis_flat[:, q * nz : (q + 1) * nz] = jnp.concatenate(
+            [basis_ref[:, q * group + i, :] for i in range(group)], axis=1
+        )
 
     for entry in level_sends:
         arrived(entry)
@@ -282,7 +303,7 @@
             carry,
         )
     mine[...] = jnp.dot(
-        basis_ref[...],
+        basis_flat[...],
         product[...],
         precision=lax.Precision.HIGHEST,
         preferred_element_type=jnp.float32,
@@ -300,9 +321,6 @@
         copy.start()
         part_copies.append(copy)
 
-    for entry in first:
-        arrived(entry)
-
     def line_of(x, width, lo_ref, hi_ref, k):
         left = x < width
         right = x >= width + nx
@@ -314,22 +332,28 @@
         lo = jnp.where(jnp.logical_and(in_col, has[("row", -1)]), lo_ref[k, x], 0.0)
         return hi, lo
 
-    def unpack(x, _):
-        for k in range(4):
-            hi, lo = line_of(x, W1, got_lo, got_hi, k)
-            field[k, x, ny : ny + 8] = jnp.concatenate([hi, lo], axis=0)
-        return 0
-
-    lax.fori_loop(0, nx + 2 * W1, unpack, 0)
-
-    @pl.when(jnp.logical_not(has[("col", -1)]))
-    def _():
-        field[:, 0:W1, 0:ny] = jnp.zeros((4, W1, ny, nz), jnp.float32)
-
-    @pl.when(jnp.logical_not(has[("col", 1)]))
-    def _():
-        field[:, nx + W1 : nx + 2 * W1, 0:ny] = jnp.zeros((4, W1, ny, nz), jnp.float32)
-
+    def take(entries, low, high):
+        for entry in entries:
+            arrived(entry)
+
+        def unpack(x, _):
+            for k in range(low, high):
+                hi, lo = line_of(x, W1, got_lo, got_hi, k)
+                field[k, x, ny : ny + 8] = jnp.concatenate([hi, lo], axis=0)
+            return 0
+
+        lax.fori_loop(0, nx + 2 * W1, unpack, 0, unroll=4)
+        blank = jnp.zeros((high - low, W1, ny, nz), jnp.float32)
+
+        @pl.when(jnp.logical_not(has[("col", -1)]))
+        def _():
+            field[low:high, 0:W1, 0:ny] = blank
+
+        @pl.when(jnp.logical_not(has[("col", 1)]))
+        def _():
+            field[low:high, nx + W1 : nx + 2 * W1, 0:ny] = blank
+
+    take(mu_sends, 3, 4)
     tall = ny + 8
     sub = lax.broadcasted_iota(jnp.int32, (tall, nz), 0)
     lane = lax.broadcasted_iota(jnp.int32, (tall, nz), 1)
@@ -358,7 +382,8 @@
             coef[slot, x] = jnp.where(inside, value, 0.0)
         return 0
 
-    lax.fori_loop(1, nx + 2 * W1 - 1, coefficients, 0)
+    lax.fori_loop(1, nx + 2 * W1 - 1, coefficients, 0, unroll=2)
+    take(first, 0, 3)
 
     def advance(src, dst, low, high, last):
         def one(x, _):
@@ -379,7 +404,7 @@
                     dst[k, x] = new
             return 0
 
-        lax.fori_loop(low, high, one, 0)
+        lax.fori_loop(low, high, one, 0, unroll=2)
 
     end = nx + 2 * W1
     advance(field, other, 1, end - 1, False)
@@ -395,7 +420,7 @@
             pack2_hi[k, x] = field[k, W1 + x, ny - 8 : ny][8 - W2 : 8]
         return 0
 
-    lax.fori_loop(0, nx, pack2, 0)
+    lax.fori_loop(0, nx, pack2, 0, unroll=4)
     second = [
         remote(pack2_hi, got2_lo.at[:, W2 : W2 + nx], 1, 0),
         remote(pack2_lo, got2_hi.at[:, W2 : W2 + nx], -1, 0),
@@ -430,14 +455,14 @@
             field[k, x + W1 - W2, ny : ny + 8] = jnp.concatenate([hi, gap, lo], axis=0)
         return 0
 
-    lax.fori_loop(0, nx + 2 * W2, unpack2, 0)
+    lax.fori_loop(0, nx + 2 * W2, unpack2, 0, unroll=4)
     for k in range(3):
         field[k, W1 - W2 : W1, 0:ny] = jnp.where(has[("col", -1)], side2_lo[k], 0.0)
         field[k, W1 + nx : W1 + nx + W2, 0:ny] = jnp.where(has[("col", 1)], side2_hi[k], 0.0)
     advance(field, other, W1 - 1, W1 + nx + 1, False)
     advance(other, mom_out, W1, W1 + nx, True)
 
-    for entry in first[:-2] + level_sends + second:
+    for entry in mu_sends + first[:-2] + level_sends + second:
         departed(entry)
     for copy in part_copies:
         copy.wait_send()
@@ -460,10 +485,9 @@
 ):
     nx, ny, nz = level_cot.shape
     ndes = design_basis.shape[0]
-    basis = design_basis.reshape(ndes, nx * ny)
     wide, tall = nx + 2 * W1, ny + 8
     f32 = jnp.float32
-    anywhere = pl.BlockSpec(memory_space=pl.ANY)
+    hbm = pl.BlockSpec(memory_space=pltpu.HBM)
     vmem = pl.BlockSpec(memory_space=pltpu.VMEM)
     smem = pl.BlockSpec(memory_space=pltpu.SMEM)
     return pl.pallas_call(
@@ -473,7 +497,7 @@
             jax.ShapeDtypeStruct((3, nx, ny, nz), f32),
             jax.ShapeDtypeStruct((1, ndes), f32),
         ),
-        in_specs=[anywhere] * 7 + [vmem, smem, vmem, vmem],
+        in_specs=[hbm] * 8 + [smem, hbm, hbm],
         out_specs=(vmem, vmem, vmem),
         scratch_shapes=[
             pltpu.VMEM((4, wide, tall, nz), f32),
@@ -495,14 +519,18 @@
             pltpu.VMEM((3, W2, ny, nz), f32),
             pltpu.VMEM((ndes, nz), f32),
             pltpu.VMEM((n_col, ndes, nz), f32),
-            pltpu.SemaphoreType.DMA((9,)),
-            pltpu.SemaphoreType.DMA((20,)),
-            pltpu.SemaphoreType.DMA((20,)),
+            pltpu.VMEM(band_cells.shape, jnp.int32),
+            pltpu.VMEM(band_force.shape, f32),
+            pltpu.VMEM(design_basis.shape, f32),
+            pltpu.VMEM((ndes, nx * ny), f32),
+            pltpu.SemaphoreType.DMA((12,)),
+            pltpu.SemaphoreType.DMA((28,)),
+            pltpu.SemaphoreType.DMA((28,)),
             pltpu.SemaphoreType.DMA((n_col,)),
             pltpu.SemaphoreType.DMA((n_col,)),
         ],
         compiler_params=pltpu.CompilerParams(
-            collective_id=0, has_side_effects=True, vmem_limit_bytes=50 * 1024 * 1024
+            collective_id=0, has_side_effects=True, vmem_limit_bytes=62 * 1024 * 1024
         ),
     )(
         level_cot,
@@ -515,7 +543,7 @@
         band_cells,
         band_count,
         band_force,
-        basis,
+        design_basis,
     )
 
 

time: 66.1 us -> 49.6 us (0.75)
  Pallas kernels: 51.3 us -> 43 us
  local copies, waits for them, and re-layouts: 12.8 us -> 5.05 us
    pallas_call x1, Pallas kernels: 51.3 us -> 43 us  [local(): pl.pallas_call(functools.partial(kernel, n_row, n_col), out_shape=(jax.Sh...]
    unnamed x19 -> x5, local copies, waits for them, and re-layouts: 11.7 us -> 5.05 us
    reshape x1 -> x0, local copies, waits for them, and re-layouts: 1.09 us -> none  [local(): basis = design_basis.reshape(ndes, nx * ny)]
where the time goes in v2:
time: 49.6 us; the launch traced here: 49.4 us
  Pallas kernels  43 us (87%)
  local copies, waits for them, and re-layouts  5.05 us (10%)
  between operations  1.29 us (3%)
    pallas_call x1, Pallas kernels, local(): pl.pallas_call(functools.partial(kernel, n_row, n_col), out_shape=(jax.Sh...  43 us
    unnamed x5, local copies, waits for them, and re-layouts  5.05 us

profile of v2, /device:TPU:9, one launch (start us, length us, event | category | flops | bytes accessed | tf_op | source)
XLA Modules:
  0.0 49.4 jit_solution(11543454234573531876)
XLA Ops:
  1.3 43.0 %shard_map.130 = (f32[32,32,128]{2,1,0:T(8,128)}, f32[3,32,32,128]{3,2,1,0:T(8,128)}, f32[1,16]{1,0:T(1,128)}) custom-call(f32[32,32,128]{2,1,0:T(8,128)} %cot_hbm.1, f32[32,32,128]{2,1,0:T(8,128)} %state_hbm.1, f32[3,32,32,128]{3,2,1,0:T(8,128)} %mom_hbm.1, f32[32,32,128]{2,1,0:T(8,128)} %courant_hbm.1, s32[32,32,128]{2,1,0:T(8,128)} %stencil_hbm.1, ...), custom_call_target="tpu_custom_call" | custom-call | tf_op jit(solution)/shard_map/pallas_call | solution.py:493
  44.3 1.9 %copy.18 = f32[32,32,128]{2,1,0:T(8,128)} copy(f32[32,32,128]{2,1,0:T(8,128)} %get-tuple-element.6) | data formatting | bytes 1048576
  46.2 0.0 copy-start
  46.2 2.7 %copy.19 = f32[3,32,32,128]{3,2,1,0:T(8,128)} copy(f32[3,32,32,128]{3,2,1,0:T(8,128)} %get-tuple-element.7) | data formatting | bytes 3145728
  48.9 0.0 copy-done
  48.9 0.5 %copy.20 = f32[1,16]{1,0:T(1,128)} copy(f32[1,16]{1,0:T(1,128)S(1)} %copy-done) | data formatting | bytes 128
Async XLA Ops:
  46.2 2.7 %copy-start = (f32[1,16]{1,0:T(1,128)S(1)}, f32[1,16]{1,0:T(1,128)}, u32[]{:S(2)}) copy-start(f32[1,16]{1,0:T(1,128)} %get-tuple-element.8) | copy-start | bytes 196

commit v3 on v2

--- a/solution.py
+++ b/solution.py
@@ -14,6 +14,7 @@
 W2 = 2
 CHUNK = 512
 FACES = 3
+EARLY = 5
 
 
 def kernel(
@@ -56,6 +57,7 @@
     force_ref,
     basis_ref,
     basis_flat,
+    cot_field,
     local_sem,
     send_sem,
     recv_sem,
@@ -113,6 +115,7 @@
     for slot, src in enumerate((stencil_hbm, upwind_hbm)):
         fetch(src, codes.at[slot, FACES : FACES + nx])
     fetch(cells_hbm, cells_ref)
+    fetch(mom_hbm, cot_field)
     fetch(force_hbm, force_ref)
     fetch(basis_hbm, basis_ref)
 
@@ -226,7 +229,9 @@
 
         return 0
 
-    lax.fori_loop(0, band_cap // CHUNK, band, 0)
+    chunks = band_cap // CHUNK
+    early = chunks * EARLY // 8
+    lax.fori_loop(0, early, band, 0)
 
     group = nz // ny
     for q in range(nx // group):
@@ -277,16 +282,7 @@
             product[pl.ds(at, ny), :] = weighted * value
         if with_out:
             j = e - 5
-            at = pl.multiple_of(j * ny, ny)
-            strength = jnp.zeros((ny, nz), jnp.float32)
-            for k in range(3):
-                force = (
-                    band_sum[pl.ds(at, ny), 2 * k * nz : (2 * k + 1) * nz]
-                    + band_sum[pl.ds(at, ny), (2 * k + 1) * nz : (2 * k + 2) * nz]
-                )
-                strength = strength + force * field[k, W1 + j, 0:ny]
-            bend = pltpu.roll(strength, 1, 1) + pltpu.roll(strength, nz - 1, 1) - 2.0 * strength
-            level_out[j] = lev[0, j + FACES] + sums[0] + bend
+            level_out[j] = lev[0, j + FACES] + sums[0]
         return tuple(sums[1:]) + (jnp.zeros((ny, nz), jnp.float32),)
 
     carry = tuple(jnp.zeros((ny, nz), jnp.float32) for _ in range(6))
@@ -404,7 +400,7 @@
                     dst[k, x] = new
             return 0
 
-        lax.fori_loop(low, high, one, 0, unroll=2)
+        lax.fori_loop(low, high, one, 0, unroll=4 if (high - low) % 4 == 0 else 2)
 
     end = nx + 2 * W1
     advance(field, other, 1, end - 1, False)
@@ -445,6 +441,23 @@
     )
     grad_out[...] = summed[0:1] / math.sqrt(n_col * nx * ny * nz)
 
+    lax.fori_loop(early, chunks, band, 0)
+
+    def tension(j, _):
+        at = pl.multiple_of(j * ny, ny)
+        strength = jnp.zeros((ny, nz), jnp.float32)
+        for k in range(3):
+            force = (
+                band_sum[pl.ds(at, ny), 2 * k * nz : (2 * k + 1) * nz]
+                + band_sum[pl.ds(at, ny), (2 * k + 1) * nz : (2 * k + 2) * nz]
+            )
+            strength = strength + force * cot_field[k, j]
+        bend = pltpu.roll(strength, 1, 1) + pltpu.roll(strength, nz - 1, 1) - 2.0 * strength
+        level_out[j] += bend
+        return 0
+
+    lax.fori_loop(0, nx, tension, 0, unroll=4)
+
     for entry in second:
         arrived(entry)
     gap = jnp.zeros((8 - 2 * W2, nz), jnp.float32)
@@ -466,6 +479,26 @@
         departed(entry)
     for copy in part_copies:
         copy.wait_send()
+
+
+def deliver(level_in, mom_in, grad_in, level_out, mom_out, grad_out, level, mom, grad, sem):
+    trips = [(grad_in, grad, grad_out)]
+    for src, mid, dst in [(level_in, level, level_out)] + [
+        (mom_in.at[k], mom.at[k], mom_out.at[k]) for k in range(3)
+    ]:
+        half = src.shape[0] // 2
+        for at in (0, half):
+            part = slice(at, at + half)
+            trips.append((src.at[part], mid.at[part], dst.at[part]))
+    loads = [pltpu.make_async_copy(a, b, sem.at[0, i]) for i, (a, b, _) in enumerate(trips)]
+    stores = [pltpu.make_async_copy(b, c, sem.at[1, i]) for i, (_, b, c) in enumerate(trips)]
+    for copy in loads:
+        copy.start()
+    for load, store in zip(loads, stores):
+        load.wait()
+        store.start()
+    for copy in stores:
+        copy.wait()
 
 
 def local(
@@ -490,7 +523,7 @@
     hbm = pl.BlockSpec(memory_space=pltpu.HBM)
     vmem = pl.BlockSpec(memory_space=pltpu.VMEM)
     smem = pl.BlockSpec(memory_space=pltpu.SMEM)
-    return pl.pallas_call(
+    made = pl.pallas_call(
         functools.partial(kernel, n_row, n_col),
         out_shape=(
             jax.ShapeDtypeStruct((nx, ny, nz), f32),
@@ -523,7 +556,8 @@
             pltpu.VMEM(band_force.shape, f32),
             pltpu.VMEM(design_basis.shape, f32),
             pltpu.VMEM((ndes, nx * ny), f32),
-            pltpu.SemaphoreType.DMA((12,)),
+            pltpu.VMEM((3, nx, ny, nz), f32),
+            pltpu.SemaphoreType.DMA((13,)),
             pltpu.SemaphoreType.DMA((28,)),
             pltpu.SemaphoreType.DMA((28,)),
             pltpu.SemaphoreType.DMA((n_col,)),
@@ -545,6 +579,15 @@
         band_force,
         design_basis,
     )
+    return pl.pallas_call(
+        deliver,
+        out_shape=tuple(jax.ShapeDtypeStruct(x.shape, x.dtype) for x in made),
+        in_specs=[hbm] * 3,
+        out_specs=(hbm,) * 3,
+        scratch_shapes=[pltpu.VMEM(x.shape, x.dtype) for x in made]
+        + [pltpu.SemaphoreType.DMA((2, 9))],
+        compiler_params=pltpu.CompilerParams(vmem_limit_bytes=62 * 1024 * 1024),
+    )(*made)
 
 
 def solution(mesh):

time: 49.6 us -> 43.1 us (0.87)
  local copies, waits for them, and re-layouts: 5.05 us -> 0 us
  Pallas kernels: 43 us -> 41.7 us
    unnamed x5 -> x0, local copies, waits for them, and re-layouts: 5.05 us -> none
    pallas_call x1, Pallas kernels: 43 us -> 39.3 us  [local(): pl.pallas_call(functools.partial(kernel, n_row, n_col), out_shape=(jax.Sh...]
    pallas_call x0 -> x1, Pallas kernels: none -> 2.42 us  [local(): pl.pallas_call(deliver, out_shape=tuple((jax.ShapeDtypeStruct(x.shape, x....]
where the time goes in v3:
time: 43.1 us; the launch traced here: 43 us
  Pallas kernels  41.7 us (97%)
  between operations  1.29 us (3%)
    pallas_call x1, Pallas kernels, local(): pl.pallas_call(functools.partial(kernel, n_row, n_col), out_shape=(jax.Sh...  39.3 us
    pallas_call x1, Pallas kernels, local(): pl.pallas_call(deliver, out_shape=tuple((jax.ShapeDtypeStruct(x.shape, x....  2.42 us

profile of v3, /device:TPU:9, one launch (start us, length us, event | category | flops | bytes accessed | tf_op | source)
XLA Modules:
  0.0 43.0 jit_solution(6719111068802438180)
XLA Ops:
  1.3 39.3 %shard_map.130 = (f32[32,32,128]{2,1,0:T(8,128)}, f32[3,32,32,128]{3,2,1,0:T(8,128)}, f32[1,16]{1,0:T(1,128)}) custom-call(f32[32,32,128]{2,1,0:T(8,128)} %cot_hbm.1, f32[32,32,128]{2,1,0:T(8,128)} %state_hbm.1, f32[3,32,32,128]{3,2,1,0:T(8,128)} %mom_hbm.1, f32[32,32,128]{2,1,0:T(8,128)} %courant_hbm.1, s32[32,32,128]{2,1,0:T(8,128)} %stencil_hbm.1, ...), custom_call_target="tpu_custom_call" | custom-call | tf_op jit(solution)/shard_map/pallas_call | solution.py:526
  40.5 2.4 %shard_map.131 = (f32[32,32,128]{2,1,0:T(8,128)}, f32[3,32,32,128]{3,2,1,0:T(8,128)}, f32[1,16]{1,0:T(1,128)}) custom-call(f32[32,32,128]{2,1,0:T(8,128)} %get-tuple-element.6.level_in, f32[3,32,32,128]{3,2,1,0:T(8,128)} %get-tuple-element.7.mom_in, f32[1,16]{1,0:T(1,128)} %get-tuple-element.8.grad_in), custom_call_target="tpu_custom_call" | custom-call | tf_op jit(solution)/shard_map/pallas_call | solution.py:582
